TPU v7x, 128 devices: a whole 4x4x4 slice. The times are simulated.
128 devices in a mesh: af: 8 (over z, y_hi), sa: 16 (over x, y_lo, core).
Axes of the slice: x: 4, y: 4 (y_hi: 2, y_lo: 2; y = y_hi * 2 + y_lo), z: 4, core: 2. Of those that a mesh axis runs over, the one named last changes fastest.
Arguments:
- tensor: bfloat16 [1024, 1024, 288], P('sa', 'af'), may hold values from -6 to 6
- omega_two: bfloat16 [1024, 256], P('sa'), may hold values from -0.1875 to 0.1875
- omega_three: bfloat16 [288, 256], replicated, may hold values from -0.375 to 0.375
- sketch_rank: bfloat16 [256, 256], P('sa'), may hold values from -0.375 to 0.375
- sketch_plane: bfloat16 [288, 256], replicated, may hold values from -0.375 to 0.375
Outputs:
- core: float32 [256, 256, 288], P('af', 'sa')
All inputs are finite; a program needn't handle non-finite values.
Results may differ from a plain program's by a relative error of at most 0.025.
Values may be sent and summed in bfloat16 or wider, within the bound.
No kernel may reach another device: no remote copies, remote signals or barrier semaphores. Data moves between devices by JAX's collectives and lax.ppermute only.
A program may use at most 128 MiB of HBM per device.

v0:
```python
import jax
import jax.numpy as jnp
from jax import lax
from jax.sharding import PartitionSpec as P

HIGH = lax.Precision.HIGHEST


def local_gram(sketch):
    return jnp.dot(sketch.T, sketch, precision=HIGH, preferred_element_type=jnp.float32)


def finish(sketch, inner_gram):
    factor = jnp.linalg.cholesky(inner_gram)
    return lax.linalg.triangular_solve(
        factor, sketch, left_side=False, lower=True, transpose_a=True
    )


def on_device(tensor, omega_two, omega_three, sketch_rank, sketch_plane):
    n_owner = lax.axis_size("af")
    local_rows = tensor.shape[0]
    plane_count = tensor.shape[2]
    rank_total = omega_two.shape[1]
    fine_rows = local_rows // n_owner
    inner = jnp.einsum("jik,kr->jir", tensor, omega_three, preferred_element_type=jnp.float32)
    sketch_terms = jnp.einsum("jr,jir->ir", omega_two.astype(jnp.float32), inner, precision=HIGH)
    first_sketch = lax.psum(sketch_terms, "sa")
    first_gram = lax.psum(local_gram(first_sketch), "af")
    basis_low = finish(first_sketch, first_gram).astype(jnp.bfloat16)
    block_terms = jnp.einsum(
        "ia,jik->jak", basis_low, tensor, preferred_element_type=jnp.float32
    ).astype(jnp.bfloat16)
    grouped = block_terms.reshape(n_owner, fine_rows, rank_total, plane_count)
    relaid = lax.all_to_all(grouped, "sa", split_axis=2, concat_axis=1, tiled=True)
    summed_rows = lax.psum_scatter(
        relaid.astype(jnp.float32).astype(jnp.bfloat16), "af", scatter_dimension=0, tiled=True
    )
    core_one = summed_rows[0]
    plane_inner = jnp.einsum(
        "jak,kr->jar", core_one, sketch_plane, preferred_element_type=jnp.float32
    )
    second_terms = jnp.einsum(
        "ar,jar->jr", sketch_rank.astype(jnp.float32), plane_inner, precision=HIGH
    )
    second_sketch = lax.psum(second_terms, "sa")
    second_gram = lax.psum(local_gram(second_sketch), "af")
    basis_high = finish(second_sketch, second_gram).astype(jnp.bfloat16)
    core_terms = jnp.einsum("jc,jak->cak", basis_high, core_one, preferred_element_type=jnp.float32)
    return lax.psum_scatter(core_terms, "af", scatter_dimension=0, tiled=True)


def solution(mesh):
    placed = (P("sa", "af", None), P("sa", None), P(), P("sa", None), P())
    return jax.shard_map(
        on_device, mesh=mesh, in_specs=placed, out_specs=P("af", "sa", None), check_vma=False
    )
```

profile of v0, /device:TPU:0, one launch (start us, length us, event | category | flops | bytes accessed | tf_op | source)
XLA Modules:
  0.0 993.4 jit_solution(16177077991976299884)
XLA Ops:
  7.5 5.4 multiply_reduce_fusion
  12.9 117.8 %all-reduce.6.cloned.1.call-done = f32[128,256]{1,0:T(8,128)} async-done(((f32[128,256]{1,0:T(8,128)}), f32[128,256]{1,0:T(8,128)}) %all-reduce.6.cloned.1.call-update) | async-done | bytes 131088 | tf_op jit(solution)/shard_map/psum | solution.py:28
  130.7 2.2 fusion.33
  133.2 85.6 %all-reduce.8.cloned.1.call-done = f32[256,256]{0,1:T(8,128)} async-done(((f32[256,256]{0,1:T(8,128)}), f32[256,256]{0,1:T(8,128)}) %all-reduce.8.cloned.1.call-update) | async-done | bytes 262160 | tf_op jit(solution)/shard_map/psum | solution.py:29
  218.9 1.1 copy.23
  221.0 11.7 %cholesky.130 = f32[128,128]{1,0:T(8,128)S(1)} custom-call(f32[128,128]{1,0:T(8,128)S(1)} %cholesky.194), custom_call_target="Cholesky" | custom-call | tf_op jit(solution)/shard_map/jit(cholesky)/cholesky | solution.py:14
  232.7 9.8 custom-call.13
  243.0 11.7 %cholesky.147 = f32[128,128]{1,0:T(8,128)S(1)} custom-call(f32[128,128]{1,0:T(8,128)S(1)} %convolution_subtract_fusion.3), custom_call_target="Cholesky" | custom-call | tf_op jit(solution)/shard_map/jit(cholesky)/cholesky | solution.py:14
  257.0 4.6 while.4
  258.1 1.4 bitcast_dynamic-update-slice_fusion.4
  260.2 1.4 bitcast_dynamic-update-slice_fusion.4
  261.6 19.7 %custom-call.14 = f32[2,128,128]{1,2,0:T(8,128)S(1)} custom-call(f32[2,128,128]{2,1,0:T(8,128)S(1)} %get-tuple-element.21), custom_call_target="InvertDiagBlocksLowerTriangular" | custom-call | tf_op jit(solution)/shard_map/triangular_solve/custom-call.0 | solution.py:15
  282.2 8.5 convolution_convert_fusion
  290.7 16.1 %copy.25 = bf16[8,8,256,288]{3,1,0,2:T(8,128)(2,1)} copy(bf16[8,8,256,288]{2,3,1,0:T(8,128)(2,1)} %bitcast.104) | data formatting | bytes 18874368 | tf_op jit(solution)/shard_map/reshape | solution.py:34
  306.9 144.4 %all_to_all.18 = bf16[8,8,256,288]{3,1,0,2:T(8,128)(2,1)S(1)} all-to-all(bf16[8,8,256,288]{3,1,0,2:T(8,128)(2,1)} %copy.25), channel_id=1, replica_groups=mesh['af'=8,'sa'=16] {'sa'}, dimensions={2} | all-to-all | bytes 18874368 | tf_op jit(solution)/shard_map/all_to_all | solution.py:35
  451.3 16.1 %copy.27 = bf16[8,16,8,16,288]{4,3,2,1,0:T(8,128)(2,1)} copy(bf16[8,16,8,16,288]{4,2,0,3,1:T(8,128)(2,1)S(1)} %bitcast.103) | data formatting | bytes 18874368 | tf_op jit(solution)/shard_map/all_to_all | solution.py:35
  468.1 148.0 %reduce-scatter.3.cloned.1.call-done = bf16[1,128,16,288]{3,2,1,0:T(8,128)(2,1)} async-done(((bf16[8,128,16,288]{3,2,1,0:T(8,128)(2,1)}), bf16[1,128,16,288]{3,2,1,0:T(8,128)(2,1)}) %reduce-scatter.3.cloned.1.call-update) | async-done | bytes 1179664 | tf_op jit(solution)/shard_map/reduce_scatter | solution.py:36
  616.1 2.9 multiply_reduce_fusion.1
  619.0 113.2 %all-reduce.10.cloned.1.call-done = f32[128,256]{1,0:T(8,128)} async-done(((f32[128,256]{1,0:T(8,128)}), f32[128,256]{1,0:T(8,128)}) %all-reduce.10.cloned.1.call-update) | async-done | bytes 131088 | tf_op jit(solution)/shard_map/psum | solution.py:46
  732.3 2.2 fusion.34
  734.7 85.6 %all-reduce.12.cloned.1.call-done = f32[256,256]{0,1:T(8,128)} async-done(((f32[256,256]{0,1:T(8,128)}), f32[256,256]{0,1:T(8,128)}) %all-reduce.12.cloned.1.call-update) | async-done | bytes 262160 | tf_op jit(solution)/shard_map/psum | solution.py:47
  820.3 1.1 copy.29
  822.4 11.7 %cholesky.164 = f32[128,128]{1,0:T(8,128)S(1)} custom-call(f32[128,128]{1,0:T(8,128)S(1)} %cholesky.197), custom_call_target="Cholesky" | custom-call | tf_op jit(solution)/shard_map/jit(cholesky)/cholesky | solution.py:14
  834.2 9.8 custom-call.15
  844.5 11.7 %cholesky.181 = f32[128,128]{1,0:T(8,128)S(1)} custom-call(f32[128,128]{1,0:T(8,128)S(1)} %convolution_subtract_fusion.1), custom_call_target="Cholesky" | custom-call | tf_op jit(solution)/shard_map/jit(cholesky)/cholesky | solution.py:14
  859.0 4.3 while.5
  859.8 1.4 bitcast_dynamic-update-slice_fusion.5
  861.9 1.4 bitcast_dynamic-update-slice_fusion.5
  863.3 19.7 %custom-call.16 = f32[2,128,128]{1,2,0:T(8,128)S(1)} custom-call(f32[2,128,128]{2,1,0:T(8,128)S(1)} %get-tuple-element.22), custom_call_target="InvertDiagBlocksLowerTriangular" | custom-call | tf_op jit(solution)/shard_map/triangular_solve/custom-call.0 | solution.py:15
  883.9 3.7 fusion
  887.6 96.3 %reduce-scatter.5.cloned.1.call-done = f32[32,16,288]{2,0,1:T(8,128)} async-done(((f32[256,16,288]{2,0,1:T(8,128)}), f32[32,16,288]{2,0,1:T(8,128)}) %reduce-scatter.5.cloned.1.call-update) | async-done | bytes 589840 | tf_op jit(solution)/shard_map/reduce_scatter | solution.py:50
  983.8 2.5 copy.31
  (65 shorter events, 11.8 us)
Async XLA Ops:
  6.5 0.9 copy-start
  6.5 124.2 %all-reduce.6.cloned.1.call-start = ((), (), s32[]{:S(2)}) async-start(), calls=%async_computation.3 | async-start | bytes 262144 | tf_op jit(solution)/shard_map/psum | solution.py:28
  12.9 206.0 %all-reduce.8.cloned.1.call-start = ((), (), s32[]{:S(2)}) async-start(), calls=%async_computation.4 | async-start | bytes 524288 | tf_op jit(solution)/shard_map/psum | solution.py:29
  130.7 150.6 %copy-start.3 = (f32[128,256]{1,0:T(8,128)S(1)}, f32[128,256]{1,0:T(8,128)}, u32[]{:S(2)}) copy-start(f32[128,256]{1,0:T(8,128)} %all-reduce.6.cloned.1.call-done) | copy-start | bytes 393220
  132.9 483.2 %reduce-scatter.3.cloned.1.call-start = ((), (), s32[]{:S(2)}) async-start(), calls=%async_computation.5 | async-start | bytes 14155776 | tf_op jit(solution)/shard_map/reduce_scatter | solution.py:36
  467.4 0.7 copy-start.5
  467.4 148.7 %copy-start.6 = (bf16[288,256]{1,0:T(8,128)(2,1)S(1)}, bf16[288,256]{1,0:T(8,128)(2,1)}, u32[]{:S(2)}) copy-start(bf16[288,256]{1,0:T(8,128)(2,1)} %param.12) | copy-start | bytes 442372
  467.4 264.8 %all-reduce.10.cloned.1.call-start = ((), (), s32[]{:S(2)}) async-start(), calls=%async_computation.6 | async-start | bytes 262144 | tf_op jit(solution)/shard_map/psum | solution.py:46
  616.1 267.8 %copy-start.2 = (bf16[1,128,16,288]{3,2,1,0:T(8,128)(2,1)S(1)}, bf16[1,128,16,288]{3,2,1,0:T(8,128)(2,1)}, u32[]{:S(2)}) copy-start(bf16[1,128,16,288]{3,2,1,0:T(8,128)(2,1)} %reduce-scatter.3.cloned.1.call-done) | copy-start | bytes 3538948
  619.0 201.3 %all-reduce.12.cloned.1.call-start = ((), (), s32[]{:S(2)}) async-start(), calls=%async_computation.7 | async-start | bytes 524288 | tf_op jit(solution)/shard_map/psum | solution.py:47
  732.3 150.7 %copy-start.4 = (f32[128,256]{1,0:T(8,128)S(1)}, f32[128,256]{1,0:T(8,128)}, u32[]{:S(2)}) copy-start(f32[128,256]{1,0:T(8,128)} %all-reduce.10.cloned.1.call-done) | copy-start | bytes 393220
  734.5 249.4 %reduce-scatter.5.cloned.1.call-start = ((), (), s32[]{:S(2)}) async-start(), calls=%async_computation.8 | async-start | bytes 7077888 | tf_op jit(solution)/shard_map/reduce_scatter | solution.py:50
  883.9 102.4 %copy-start.1 = (bf16[288,256]{1,0:T(8,128)(2,1)S(1)}, bf16[288,256]{1,0:T(8,128)(2,1)}, u32[]{:S(2)}) copy-start(bf16[288,256]{1,0:T(8,128)(2,1)} %param.10) | copy-start | bytes 442372
Sparse Core Ops, SparseCore 0:
  13.0 117.6 all-reduce.5
  133.3 85.5 all-reduce.7
  467.5 148.4 reduce-scatter.2
  619.1 113.1 all-reduce.9
  734.7 85.5 all-reduce.11
  887.7 96.0 reduce-scatter.4
where the time goes:
time: 997 us; the launch traced here: 993 us
  waiting for transfers between devices  647 us (65%)
  blocking collectives  144 us (14%)
  other arithmetic  111 us (11%)
  local copies, waits for them, and re-layouts  45.9 us (5%)
  matrix products  27.5 us (3%)
  between operations  16.6 us (2%)
    reduce_scatter x1, waiting for transfers between devices, on_device(): lax.psum_scatter(relaid.astype(jnp.float32).astype(jnp.bfloat16), 'af', s...  148 us
    all_to_all x1, blocking collectives, on_device(): lax.all_to_all(grouped, 'sa', split_axis=2, concat_axis=1, tiled=True)  144 us
    psum x1, waiting for transfers between devices, on_device(): first_sketch = lax.psum(sketch_terms, 'sa')  118 us
    psum x1, waiting for transfers between devices, on_device(): second_sketch = lax.psum(second_terms, 'sa')  113 us
    reduce_scatter x1, waiting for transfers between devices, on_device(): return lax.psum_scatter(core_terms, 'af', scatter_dimension=0, tiled=True)  96.3 us
    psum x1, waiting for transfers between devices, on_device(): first_gram = lax.psum(local_gram(first_sketch), 'af')  85.6 us
    psum x1, waiting for transfers between devices, on_device(): second_gram = lax.psum(local_gram(second_sketch), 'af')  85.6 us
    another operation x13, other arithmetic, finish(): factor = jnp.linalg.cholesky(inner_gram)  68.7 us
  transfers between devices with their start and end apart: 6, of which 6 were waited for; matrix products, arithmetic and copies ran while one was open for 0% of the time, Pallas kernels for 0%

commit v1 on v0

v1 whole, which is shorter than its diff:
```python
import jax
import jax.numpy as jnp
from jax import lax
from jax.sharding import PartitionSpec as P

HIGH = lax.Precision.HIGHEST


def orthonormal(sketch):
    gram = jnp.dot(sketch.T, sketch, precision=HIGH, preferred_element_type=jnp.float32)
    factor = jnp.linalg.cholesky(gram)
    return lax.linalg.triangular_solve(
        factor, sketch, left_side=False, lower=True, transpose_a=True
    )


def exchange(blocks, axes):
    return lax.all_to_all(blocks, axes, split_axis=0, concat_axis=0, tiled=True)


def gather(rows, axes, count):
    shared = jnp.broadcast_to(rows[None], (count,) + rows.shape)
    return exchange(shared, axes).reshape(count * rows.shape[0], rows.shape[1])


def on_device(tensor, omega_two, omega_three, sketch_rank, sketch_plane):
    n_af = lax.axis_size("af")
    n_sa = lax.axis_size("sa")
    n_all = n_af * n_sa
    local_rows, local_cols, planes = tensor.shape
    rank = omega_two.shape[1]
    fine_rows = local_rows // n_af
    fine_cols = local_cols // n_sa

    moved = exchange(tensor.reshape(n_af, fine_rows, local_cols, planes), "af")

    inner = jnp.einsum("jik,kr->jir", tensor, omega_three, preferred_element_type=jnp.float32)
    terms = jnp.einsum("jr,jir->ir", omega_two.astype(jnp.float32), inner, precision=HIGH)
    parts = exchange(terms.reshape(n_sa, fine_cols, rank), "sa")
    first_sketch = gather(jnp.sum(parts, axis=0), ("af", "sa"), n_all)
    basis_low = orthonormal(first_sketch).astype(jnp.bfloat16)

    core_one = jnp.einsum(
        "pjik,pia->jak",
        moved,
        basis_low.reshape(n_af, local_cols, rank),
        preferred_element_type=jnp.float32,
    ).astype(jnp.bfloat16)

    plane_inner = jnp.einsum(
        "jak,kr->jar", core_one, sketch_plane, preferred_element_type=jnp.float32
    )
    whole_rank = gather(sketch_rank, "sa", n_sa)
    second_rows = jnp.einsum(
        "ar,jar->jr", whole_rank.astype(jnp.float32), plane_inner, precision=HIGH
    )
    second_sketch = gather(second_rows, ("sa", "af"), n_all)

    share = rank // n_all
    split = core_one.reshape(fine_rows, n_all, share * planes).transpose(1, 0, 2)
    columns = exchange(split, ("sa", "af")).reshape(n_all * fine_rows, share * planes)

    basis_high = orthonormal(second_sketch).astype(jnp.bfloat16)
    core = jnp.dot(basis_high.T, columns, preferred_element_type=jnp.float32)
    swapped = exchange(core.reshape(n_af, rank // n_af, share * planes), "af")
    swapped = swapped.reshape(n_af, rank // n_af, share, planes)
    return swapped.transpose(1, 0, 2, 3).reshape(rank // n_af, n_af * share, planes)


def solution(mesh):
    placed = (P("sa", "af", None), P("sa", None), P(), P("sa", None), P())
    return jax.shard_map(
        on_device, mesh=mesh, in_specs=placed, out_specs=P("af", "sa", None), check_vma=False
    )
```

time: 997 us -> 258 us (0.26)
  waiting for transfers between devices: 647 us -> 21 us
  blocking collectives: 144 us -> 59.3 us
  local copies, waits for them, and re-layouts: 45.9 us -> 16.3 us
  starting transfers between devices: 0.67 us -> 22.5 us
  between operations: 16.6 us -> 3.39 us
    psum x4 -> x0, waiting for transfers between devices: 402 us -> none  [the longest x1 118 us: on_device(): first_sketch = lax.psum(sketch_terms, 'sa')]
    reduce_scatter x2 -> x0, waiting for transfers between devices: 244 us -> none  [the longest x1 148 us: on_device(): lax.psum_scatter(relaid.astype(jnp.float32).astype(jnp.bfloat16), 'af', s...]
    all_to_all x1 -> x3, blocking collectives: 144 us -> 59.3 us  [exchange(): return lax.all_to_all(blocks, axes, split_axis=0, concat_axis=0, tiled=True)]
    all_to_all x0 -> x4, starting transfers between devices: none -> 22.5 us  [exchange(): return lax.all_to_all(blocks, axes, split_axis=0, concat_axis=0, tiled=True)]
    all_to_all x0 -> x4, waiting for transfers between devices: none -> 21 us  [exchange(): return lax.all_to_all(blocks, axes, split_axis=0, concat_axis=0, tiled=True)]
    all_to_all x1 -> x0, local copies, waits for them, and re-layouts: 16.1 us -> none  [on_device(): lax.all_to_all(grouped, 'sa', split_axis=2, concat_axis=1, tiled=True)]
    reshape x1 -> x4, local copies, waits for them, and re-layouts: 16.1 us -> 3.26 us  [the longest x1 1.42 us: on_device(): swapped.transpose(1, 0, 2, 3).reshape(rank // n_af, n_af * share, planes)]
  transfers between devices with their start and end apart: 6 -> 4, of which waited for: 6 -> 2; matrix products, arithmetic and copies ran while one was open for 0% -> 52% of each run, Pallas kernels for 0% -> 0%
where the time goes in v1:
time: 258 us; the launch traced here: 254 us
  other arithmetic  109 us (42%)
  blocking collectives  59.3 us (23%)
  matrix products  22.6 us (9%)
  starting transfers between devices  22.5 us (9%)
  waiting for transfers between devices  21 us (8%)
  local copies, waits for them, and re-layouts  16.3 us (6%)
  between operations  3.39 us (1%)
    another operation x13, other arithmetic, orthonormal(): factor = jnp.linalg.cholesky(gram)  68.6 us
    all_to_all x3, blocking collectives, exchange(): return lax.all_to_all(blocks, axes, split_axis=0, concat_axis=0, tiled=True)  59.3 us
    another operation x5, other arithmetic, orthonormal(): lax.linalg.triangular_solve(factor, sketch, left_side=False, lower=True,...  39.4 us
    all_to_all x4, starting transfers between devices, exchange(): return lax.all_to_all(blocks, axes, split_axis=0, concat_axis=0, tiled=True)  22.5 us
    all_to_all x4, waiting for transfers between devices, exchange(): return lax.all_to_all(blocks, axes, split_axis=0, concat_axis=0, tiled=True)  21 us
    another operation x15, local copies, waits for them, and re-layouts, orthonormal(): lax.linalg.triangular_solve(factor, sketch, left_side=False, lower=True,...  7.91 us
    another operation x6, matrix products, orthonormal(): lax.linalg.triangular_solve(factor, sketch, left_side=False, lower=True,...  6.6 us
    dot_general x2, matrix products, orthonormal(): jnp.dot(sketch.T, sketch, precision=HIGH, preferred_element_type=jnp.floa...  5.24 us
  transfers between devices with their start and end apart: 4, of which 2 were waited for; matrix products, arithmetic and copies ran while one was open for 52% of the time, Pallas kernels for 0%

profile of v1, /device:TPU:0, one launch (start us, length us, event | category | flops | bytes accessed | tf_op | source)
XLA Modules:
  0.0 254.2 jit_solution(3753971702710589500)
XLA Ops:
  0.9 4.7 %multiply_reduce_fusion = f32[256,128]{0,1:T(8,128)S(1)} fusion(f32[256,64]{0,1:T(8,128)S(1)} %bitcast_convert_fusion.2, bf16[64,128,288]{1,2,0:T(8,128)(2,1)} %param.8, bf16[288,256]{1,0:T(8,128)(2,1)S(1)} %copy-done), kind=kOutput, calls=%fused_computation.4 | convolution fusion | flops 1212121088 | bytes 5062656 | tf_op jit(solution)/shard_map/jik,kr->jir/dot_general | solution.py:37
  5.7 11.8 %all_to_all.35 = f32[16,8,256]{2,1,0:T(8,128)S(1)} all-to-all(f32[16,8,256]{2,1,0:T(8,128)S(1)} %bitcast.133), channel_id=1, replica_groups=mesh['af'=8,'sa'=16] {'sa'}, dimensions={0} | all-to-all | bytes 262144 | tf_op jit(solution)/shard_map/all_to_all | solution.py:18
  18.1 3.5 %all-to-all-start.3 = ((bf16[16,16,256]{2,1,0:T(8,128)(2,1)}), bf16[16,16,256]{2,1,0:T(8,128)(2,1)S(1)}, u32[]{:S(2)}, u32[]{:S(2)}) async-start(bf16[16,16,256]{2,1,0:T(8,128)(2,1)} %broadcast_in_dim.8), calls=%async_computation.3 | async-start | bytes 262144 | tf_op jit(solution)/shard_map/all_to_all | solution.py:18
  21.7 6.4 %all-to-all-done.3 = bf16[16,16,256]{2,1,0:T(8,128)(2,1)S(1)} async-done(((bf16[16,16,256]{2,1,0:T(8,128)(2,1)}), bf16[16,16,256]{2,1,0:T(8,128)(2,1)S(1)}, u32[]{:S(2)}, u32[]{:S(2)}) %all-to-all-start.3) | async-done | bytes 131104 | tf_op jit(solution)/shard_map/all_to_all | solution.py:18
  28.1 27.6 %all_to_all.36 = f32[128,8,256]{2,1,0:T(8,128)S(1)} all-to-all(f32[128,8,256]{2,1,0:T(8,128)S(1)} %broadcast_in_dim.7), channel_id=1, replica_groups=mesh['af'=8,'sa'=16] {'af','sa'}, dimensions={0} | all-to-all | bytes 2097152 | tf_op jit(solution)/shard_map/all_to_all | solution.py:18
  55.8 4.8 %all-to-all-start.2 = ((bf16[8,8,128,288]{2,3,1,0:T(8,128)(2,1)}), bf16[8,8,128,288]{2,3,1,0:T(8,128)(2,1)}, u32[]{:S(2)}, u32[]{:S(2)}) async-start(bf16[8,8,128,288]{2,3,1,0:T(8,128)(2,1)} %bitcast.127), calls=%async_computation.2 | async-start | bytes 9437184 | tf_op jit(solution)/shard_map/all_to_all | solution.py:18
  60.6 1.8 convolution_bitcast_fusion.1
  62.6 11.7 %cholesky.130 = f32[128,128]{1,0:T(8,128)S(1)} custom-call(f32[128,128]{1,0:T(8,128)S(1)} %cholesky.194), custom_call_target="Cholesky" | custom-call | tf_op jit(solution)/shard_map/jit(cholesky)/cholesky | solution.py:11
  74.4 9.8 %custom-call.13 = f32[1,128,128]{1,2,0:T(8,128)S(1)} custom-call(f32[1,128,128]{2,1,0:T(8,128)S(1)} %get-tuple-element.50), custom_call_target="InvertDiagBlocksLowerTriangular" | custom-call | tf_op jit(solution)/shard_map/jit(cholesky)/cholesky | solution.py:11
  84.7 11.7 %cholesky.147 = f32[128,128]{1,0:T(8,128)S(1)} custom-call(f32[128,128]{1,0:T(8,128)S(1)} %convolution_subtract_fusion.3), custom_call_target="Cholesky" | custom-call | tf_op jit(solution)/shard_map/jit(cholesky)/cholesky | solution.py:11
  98.7 4.2 %while.4 = (s32[]{:T(128)}, f32[256,256]{1,0:T(8,128)S(1)}, s32[2,2]{1,0:T(2,128)S(1)}, f32[2,128,128]{2,1,0:T(8,128)S(1)}, s32[]{:T(128)}) while((s32[]{:T(128)}, f32[256,256]{1,0:T(8,128)S(1)}, s32[2,2]{1,0:T(2,128)S(1)}, f32[2,128,128]{2,1,0:T(8,128)S(1)}, s32[]{:T(128)}) %tuple.43), condition=%wide.while_cond, body=%wide.while_body.sunk | while | flops 2 | bytes 131181 | solution.py:12
  99.4 1.4 bitcast_dynamic-update-slice_fusion.4
  101.5 1.4 bitcast_dynamic-update-slice_fusion.4
  102.9 19.7 %custom-call.14 = f32[2,128,128]{1,2,0:T(8,128)S(1)} custom-call(f32[2,128,128]{2,1,0:T(8,128)S(1)} %get-tuple-element.21), custom_call_target="InvertDiagBlocksLowerTriangular" | custom-call | tf_op jit(solution)/shard_map/triangular_solve/custom-call.0 | solution.py:12
  125.1 3.8 %fusion = bf16[8,256,288]{1,2,0:T(8,128)(2,1)S(1)} fusion(bf16[8,128,256,1]{2,1,3,0:T(8,128)(2,1)S(1)} %bitcast.132, bf16[8,8,128,288]{2,3,1,0:T(8,128)(2,1)} %all-to-all-done.2), kind=kOutput, calls=%fused_computation.7 | convolution fusion | flops 1208549376 | bytes 6422528 | tf_op jit(solution)/shard_map/pjik,pia->jak/dot_general | solution.py:43
  130.7 9.2 %all-to-all-start.4 = ((f32[128,8,256]{2,1,0:T(8,128)}), f32[128,8,256]{2,1,0:T(8,128)}, u32[]{:S(2)}, u32[]{:S(2)}) async-start(f32[128,8,256]{2,1,0:T(8,128)} %broadcast_in_dim.9), calls=%async_computation.4 | async-start | bytes 2097152 | tf_op jit(solution)/shard_map/all_to_all | solution.py:18
  140.8 1.1 reshape.58
  141.9 1.8 copy.33
  143.7 14.6 %all-to-all-done.4 = f32[128,8,256]{2,1,0:T(8,128)} async-done(((f32[128,8,256]{2,1,0:T(8,128)}), f32[128,8,256]{2,1,0:T(8,128)}, u32[]{:S(2)}, u32[]{:S(2)}) %all-to-all-start.4) | async-done | bytes 1048608 | tf_op jit(solution)/shard_map/all_to_all | solution.py:18
  158.2 5.0 %all-to-all-start.5 = ((bf16[128,8,576]{2,1,0:T(8,128)(2,1)}), bf16[128,8,576]{2,1,0:T(8,128)(2,1)S(1)}, u32[]{:S(2)}, u32[]{:S(2)}) async-start(bf16[128,8,576]{2,1,0:T(8,128)(2,1)} %copy.33), calls=%async_computation.5 | async-start | bytes 2621440 | tf_op jit(solution)/shard_map/all_to_all | solution.py:18
  163.3 3.4 %convolution_bitcast_fusion = f32[256,256]{1,0:T(8,128)S(1)} fusion(f32[128,8,256]{2,1,0:T(8,128)} %all-to-all-done.4), kind=kOutput, calls=%fused_computation.12 | convolution fusion | flops 805306368 | bytes 1310720 | tf_op jit(solution)/shard_map/dot_general | solution.py:10
  166.9 11.7 %cholesky.164 = f32[128,128]{1,0:T(8,128)S(1)} custom-call(f32[128,128]{1,0:T(8,128)S(1)} %cholesky.197), custom_call_target="Cholesky" | custom-call | tf_op jit(solution)/shard_map/jit(cholesky)/cholesky | solution.py:11
  178.6 9.8 %custom-call.15 = f32[1,128,128]{1,2,0:T(8,128)S(1)} custom-call(f32[1,128,128]{2,1,0:T(8,128)S(1)} %get-tuple-element.46), custom_call_target="InvertDiagBlocksLowerTriangular" | custom-call | tf_op jit(solution)/shard_map/jit(cholesky)/cholesky | solution.py:11
  188.9 11.7 %cholesky.181 = f32[128,128]{1,0:T(8,128)S(1)} custom-call(f32[128,128]{1,0:T(8,128)S(1)} %convolution_subtract_fusion.2), custom_call_target="Cholesky" | custom-call | tf_op jit(solution)/shard_map/jit(cholesky)/cholesky | solution.py:11
  203.4 3.8 %while.5 = (s32[]{:T(128)}, f32[256,256]{1,0:T(8,128)S(1)}, s32[2,2]{1,0:T(2,128)S(1)}, f32[2,128,128]{2,1,0:T(8,128)S(1)}, s32[]{:T(128)}) while((s32[]{:T(128)}, f32[256,256]{1,0:T(8,128)S(1)}, s32[2,2]{1,0:T(2,128)S(1)}, f32[2,128,128]{2,1,0:T(8,128)S(1)}, s32[]{:T(128)}) %tuple.49), condition=%wide.while_cond.clone, body=%wide.while_body.clone.sunk | while | flops 2 | bytes 131181 | solution.py:12
  204.0 1.3 bitcast_dynamic-update-slice_fusion.5
  205.8 1.3 bitcast_dynamic-update-slice_fusion.5
  207.1 19.7 %custom-call.16 = f32[2,128,128]{1,2,0:T(8,128)S(1)} custom-call(f32[2,128,128]{2,1,0:T(8,128)S(1)} %get-tuple-element.22), custom_call_target="InvertDiagBlocksLowerTriangular" | custom-call | tf_op jit(solution)/shard_map/triangular_solve/custom-call.0 | solution.py:12
  226.8 1.7 fusion.3
  228.5 2.0 convolution_subtract_fusion
  231.8 19.9 %all_to_all.37 = f32[8,32,576]{2,1,0:T(8,128)S(1)} all-to-all(f32[8,32,576]{2,1,0:T(8,128)S(1)} %fusion.1), channel_id=1, replica_groups=mesh['af'=8,'sa'=16] {'af'}, dimensions={0} | all-to-all | bytes 1179648 | tf_op jit(solution)/shard_map/all_to_all | solution.py:18
  252.6 1.4 reshape.61
  (59 shorter events, 15.1 us)
Async XLA Ops:
  0.0 0.9 copy-start
  0.9 16.5 %copy-start.1 = (bf16[16,256]{1,0:T(8,128)(2,1)S(1)}, bf16[16,256]{1,0:T(8,128)(2,1)}, u32[]{:S(2)}) copy-start(bf16[16,256]{1,0:T(8,128)(2,1)} %param.11) | copy-start | bytes 24580
  18.1 10.0 %all-to-all-start.3 = ((bf16[16,16,256]{2,1,0:T(8,128)(2,1)}), bf16[16,16,256]{2,1,0:T(8,128)(2,1)S(1)}, u32[]{:S(2)}, u32[]{:S(2)}) async-start(bf16[16,16,256]{2,1,0:T(8,128)(2,1)} %broadcast_in_dim.8), calls=%async_computation.3 | async-start | bytes 262144 | tf_op jit(solution)/shard_map/all_to_all | solution.py:18
  55.8 69.4 %all-to-all-start.2 = ((bf16[8,8,128,288]{2,3,1,0:T(8,128)(2,1)}), bf16[8,8,128,288]{2,3,1,0:T(8,128)(2,1)}, u32[]{:S(2)}, u32[]{:S(2)}) async-start(bf16[8,8,128,288]{2,3,1,0:T(8,128)(2,1)} %bitcast.127), calls=%async_computation.2 | async-start | bytes 9437184 | tf_op jit(solution)/shard_map/all_to_all | solution.py:18
  125.1 3.8 %copy-start.2 = (bf16[288,256]{1,0:T(8,128)(2,1)S(1)}, bf16[288,256]{1,0:T(8,128)(2,1)}, u32[]{:S(2)}) copy-start(bf16[288,256]{1,0:T(8,128)(2,1)} %param.12) | copy-start | bytes 442372
  130.7 27.5 %all-to-all-start.4 = ((f32[128,8,256]{2,1,0:T(8,128)}), f32[128,8,256]{2,1,0:T(8,128)}, u32[]{:S(2)}, u32[]{:S(2)}) async-start(f32[128,8,256]{2,1,0:T(8,128)} %broadcast_in_dim.9), calls=%async_computation.4 | async-start | bytes 2097152 | tf_op jit(solution)/shard_map/all_to_all | solution.py:18
  158.2 73.0 %all-to-all-start.5 = ((bf16[128,8,576]{2,1,0:T(8,128)(2,1)}), bf16[128,8,576]{2,1,0:T(8,128)(2,1)S(1)}, u32[]{:S(2)}, u32[]{:S(2)}) async-start(bf16[128,8,576]{2,1,0:T(8,128)(2,1)} %copy.33), calls=%async_computation.5 | async-start | bytes 2621440 | tf_op jit(solution)/shard_map/all_to_all | solution.py:18

commit v2 on v1

v2 whole, which is shorter than its diff:
```python
import jax
import jax.numpy as jnp
from jax import lax
from jax.experimental import pallas as pl
from jax.experimental.pallas import tpu as pltpu
from jax.sharding import Mesh
from jax.sharding import PartitionSpec as P

HIGH = lax.Precision.HIGHEST


NT = (((1,), (1,)), ((), ()))
NN = (((1,), (0,)), ((), ()))
TN = (((0,), (0,)), ((), ()))


def mm(a, b, dims=NN, precision=None):
    return lax.dot_general(a, b, dims, precision=precision, preferred_element_type=jnp.float32)


def low(x):
    return x.astype(jnp.bfloat16)


def inverse_factor(s, basis_ref, a_ref, m_ref):
    n = s.shape[1]
    row = lax.broadcasted_iota(jnp.int32, (n, n), 0)
    col = lax.broadcasted_iota(jnp.int32, (n, n), 1)
    eye = row == col
    one = jnp.where(eye, 1.0, 0.0)
    half = jnp.where(row > col, 1.0, 0.5 * one)
    gram = mm(s, s, TN, HIGH)
    on_diag = jnp.where(eye, gram, 0.0)
    inv_row = 0.9 * lax.rsqrt(jnp.sum(on_diag, axis=0, keepdims=True))
    inv_col = 0.9 * lax.rsqrt(jnp.sum(on_diag, axis=1, keepdims=True))
    scaled = gram * inv_col * inv_row

    h = scaled
    m = None
    early = 2
    for step in range(early):
        f = half * (h - one)
        fb = low(f)
        kb = low(one - f + half * mm(fb, fb, NT) + mm(fb, fb))
        m = kb if m is None else low(mm(kb, m))
        if step < early - 1:
            h = mm(low(mm(kb, low(h))), kb, NT)
    m = m.astype(jnp.float32)
    for _ in range(2):
        r = mm(mm(m, scaled, NN, HIGH), m, NT, HIGH) - one
        m = m - mm(half * r, m, NN, HIGH)
    good = jnp.logical_and(jnp.sum(r * r) < 1e-3, jnp.min(jnp.where(eye, m, 1.0)) > 0.0)
    basis_ref[...] = low(mm(m * inv_row, s, NT, HIGH))

    @pl.when(jnp.logical_not(good))
    def _():
        a_ref[...] = scaled
        m_ref[...] = one

        def step(j, carry):
            a = a_ref[...]
            pivot_row = a_ref[pl.ds(j, 1), :]
            unit_row = m_ref[pl.ds(j, 1), :]
            column = jnp.sum(jnp.where(col == j, a, 0.0), axis=1, keepdims=True)
            pivot = jnp.sum(jnp.where(col[:1] == j, pivot_row, 0.0), axis=1, keepdims=True)
            f = jnp.where(row[:, :1] > j, column / pivot, 0.0)
            a_ref[...] = a - f * pivot_row
            m_ref[...] = m_ref[...] - f * unit_row
            return carry

        lax.fori_loop(0, n, step, 0)
        pivots = jnp.sum(jnp.where(eye, a_ref[...], 0.0), axis=1, keepdims=True)
        direct = m_ref[...] * lax.rsqrt(pivots) * inv_row
        basis_ref[...] = low(mm(direct, s, NT, HIGH))


VMEM = pl.BlockSpec(memory_space=pltpu.VMEM)
PARAMS = pltpu.CompilerParams(vmem_limit_bytes=32 * 1024 * 1024)


def cost(flops, size):
    return pl.CostEstimate(flops=flops, bytes_accessed=size, transcendentals=0)


def first_basis_kernel(s_ref, basis_ref, a_ref, m_ref):
    places = [
        ((c * 2 + yh) * 2 + yl) * 4 + z
        for z in range(4)
        for yh in range(2)
        for c in range(2)
        for yl in range(2)
    ]
    s = jnp.concatenate([s_ref[place * 32 : place * 32 + 32] for place in places], axis=0)
    inverse_factor(s, basis_ref, a_ref, m_ref)


def first_basis(sketch):
    n = sketch.shape[1]
    return pl.pallas_call(
        first_basis_kernel,
        out_shape=jax.ShapeDtypeStruct(sketch.shape[::-1], jnp.bfloat16),
        in_specs=[VMEM],
        out_specs=VMEM,
        scratch_shapes=[pltpu.VMEM((n, n), jnp.float32)] * 2,
        compiler_params=PARAMS,
        cost_estimate=cost(4 * 10**9, 2 * 10**6),
        name="first_basis",
    )(sketch)


def second_core_kernel(got_ref, other_ref, core_ref, basis_ref, a_ref, m_ref):
    lanes = core_ref.shape[1]
    sketch = got_ref[:, lanes:].astype(jnp.float32) + other_ref[...].astype(jnp.float32)
    inverse_factor(sketch, basis_ref, a_ref, m_ref)
    core_ref[...] = mm(basis_ref[...], got_ref[:, :lanes]).astype(core_ref.dtype)


def second_core(got, other):
    n = other.shape[1]
    lanes = got.shape[1] - n
    return pl.pallas_call(
        second_core_kernel,
        out_shape=jax.ShapeDtypeStruct((n, lanes), jnp.bfloat16),
        in_specs=[VMEM] * 2,
        out_specs=VMEM,
        scratch_shapes=[pltpu.VMEM((n, got.shape[0]), jnp.bfloat16)]
        + [pltpu.VMEM((n, n), jnp.float32)] * 2,
        compiler_params=PARAMS,
        cost_estimate=cost(4 * 10**9, 3 * 10**6),
        name="second_core",
    )(got, other)


def project_kernel(basis_ref, plane_ref, rank_ref, moved_ref, split_ref, core_ref):
    count, rows, planes, _ = moved_ref.shape
    rank = basis_ref.shape[0]
    basis = basis_ref[...]
    weight = rank_ref[...].astype(jnp.float32)
    sketch = []
    for j in range(rows):
        slab = jnp.concatenate([moved_ref[b, j] for b in range(count)], axis=1)
        core = low(mm(basis, slab, NT))
        core_ref[j] = core
        inner = mm(core, plane_ref[...])
        sketch.append(jnp.sum(inner * weight, axis=0, keepdims=True))
    sketch = jnp.concatenate(sketch, axis=0)
    upper = low(sketch)
    lower = low(sketch - upper.astype(jnp.float32))
    copies = 64 // rows
    halves = jnp.concatenate([upper] * copies + [lower] * copies, axis=0)

    group = 256 // rows
    pairs = group // 2
    target = lax.broadcasted_iota(jnp.int32, (256, 256), 0)
    source = lax.broadcasted_iota(jnp.int32, (256, 256), 1)
    wanted = (target % rows) * group + 2 * ((target // rows) % pairs) + target // (rows * pairs)
    permute = low(jnp.where(source == wanted, 1.0, 0.0))
    full = planes // 128 * 128
    for g in range(rank // group):
        mixed = jnp.concatenate([core_ref[j, g * group : (g + 1) * group] for j in range(rows)], 0)
        moved = low(mm(permute, mixed))
        even, odd = moved[:128], moved[128:]
        split_ref[g * 128 : (g + 1) * 128] = jnp.concatenate(
            [
                even[:, :full],
                odd[:, :full],
                even[:, full:],
                odd[:, full:],
                jnp.zeros((128, 128 - 2 * (planes - full)), jnp.bfloat16),
                halves,
            ],
            axis=1,
        )


def project(basis, sketch_plane, sketch_rank, moved):
    rows, planes = moved.shape[1:3]
    rank = basis.shape[0]
    lanes = 2 * (planes // 128) * 128 + 128
    return pl.pallas_call(
        project_kernel,
        out_shape=jax.ShapeDtypeStruct((rank // 2 * rows, lanes + rank), jnp.bfloat16),
        in_specs=[VMEM] * 4,
        out_specs=VMEM,
        scratch_shapes=[pltpu.VMEM((rows, rank, planes), jnp.bfloat16)],
        compiler_params=PARAMS,
        cost_estimate=cost(2 * 10**9, 8 * 10**6),
        name="project",
    )(basis, sketch_plane, sketch_rank, moved)


def exchange(blocks, axes):
    return lax.all_to_all(blocks, axes, split_axis=0, concat_axis=0, tiled=True)


def around(block, axes, step):
    count = lax.axis_size(axes)
    return lax.ppermute(block, axes, [(p, (p + step) % count) for p in range(count)])


def ordered(blocks, place):
    count = len(blocks)
    turned = jnp.stack(blocks[::-1] * 2)
    return lax.dynamic_slice_in_dim(turned, count - 1 - place, count, 0)


def collect(block, axes):
    count = lax.axis_size(axes)
    blocks = [block] + [around(block, axes, step) for step in range(1, count)]
    every = ordered(blocks, lax.axis_index(axes))
    return every.reshape((-1,) + block.shape[1:])


def reduce_rows(rows, extra, axes):
    count, me = lax.axis_size(axes), lax.axis_index(axes)
    shares = rows.reshape((count, -1) + rows.shape[1:])
    size = shares.shape[1]
    total = lax.dynamic_index_in_dim(shares, me, 0, keepdims=False)
    extras = [extra]
    for step in range(1, count):
        share = lax.dynamic_index_in_dim(shares, (me + step) % count, 0, keepdims=False)
        got = around(jnp.concatenate([share, extra], axis=0), axes, step)
        total = total + got[:size]
        extras.append(got[size:])
    return total, ordered(extras, me).reshape((-1,) + extra.shape[1:])


AF = ("z", "yh")
SA = ("x", "yl", "c")


def on_device(tensor, omega_two, omega_three, sketch_rank, sketch_plane):
    n_af = lax.axis_size(AF)
    n_sa = lax.axis_size(SA)
    n_all = n_af * n_sa
    local_rows, local_cols, planes = tensor.shape
    rank = omega_two.shape[1]
    fine_rows = local_rows // n_af

    inner = jnp.einsum("jik,kr->jir", tensor, omega_three, preferred_element_type=jnp.float32)
    rows = jnp.einsum("jr,jir->ir", omega_two.astype(jnp.float32), inner, precision=HIGH)
    extra = sketch_rank.astype(jnp.float32)
    for axis in ("c", "yl"):
        rows, extra = reduce_rows(rows, extra, axis)

    rows, tensor = lax.optimization_barrier((rows, tensor))
    pieces = jnp.swapaxes(tensor, 1, 2).reshape(n_af, fine_rows, planes, local_cols)
    moved = exchange(pieces, AF)
    rows, extra = reduce_rows(rows, extra, "x")
    whole_rank = extra.reshape(rank, rank)
    rows = collect(collect(rows, "x"), "z")
    rows, moved = lax.optimization_barrier((rows, moved))
    rows = collect(collect(rows, ("yh", "yl")), "c")
    basis_low = first_basis(rows)

    split = project(basis_low, sketch_plane, whole_rank, moved)
    got = exchange(split.reshape(n_all, fine_rows, -1), SA + AF).reshape(n_all * fine_rows, -1)
    core = second_core(got, around(got[:, -rank:], "c", 1))

    swapped = exchange(core.reshape(n_af, rank // n_af, -1), AF).astype(jnp.float32)
    full = planes // 128 * 128
    rest = planes - full
    even = jnp.concatenate([swapped[..., :full], swapped[..., 2 * full : 2 * full + rest]], -1)
    odd = jnp.concatenate(
        [swapped[..., full : 2 * full], swapped[..., 2 * full + rest : 2 * planes]], -1
    )
    both = jnp.stack([even, odd], axis=2)
    return both.transpose(1, 0, 2, 3).reshape(rank // n_af, 2 * n_af, planes)


def solution(mesh):
    grid = Mesh(mesh.devices.reshape(4, 2, 4, 2, 2), ("z", "yh", "x", "yl", "c"))
    placed = (P(SA, AF, None), P(SA, None), P(), P(SA, None), P())
    return jax.shard_map(
        on_device, mesh=grid, in_specs=placed, out_specs=P(AF, SA, None), check_vma=False
    )
```

time: 258 us -> 163 us (0.63); the launches traced: 254 us -> 162 us
  other arithmetic: 109 us -> 1.95 us
  waiting for transfers between devices: 21 us -> 58.2 us
  Pallas kernels: 0 us -> 19.8 us
  matrix products: 22.6 us -> 4.73 us
  blocking collectives: 59.3 us -> 44.3 us
  local copies, waits for them, and re-layouts: 16.3 us -> 2.56 us
  starting transfers between devices: 22.5 us -> 30.2 us
  between operations: 3.39 us -> 0.47 us
    another operation x18 -> x6, other arithmetic: 108 us -> 1.07 us  [the longest x5 1.01 us: ordered(): turned = jnp.stack(blocks[::-1] * 2)]
    ppermute x0 -> x16, waiting for transfers between devices: none -> 55.6 us  [around(): lax.ppermute(block, axes, [(p, (p + step) % count) for p in range(count)])]
    ppermute x0 -> x16, starting transfers between devices: none -> 22.3 us  [around(): lax.ppermute(block, axes, [(p, (p + step) % count) for p in range(count)])]
    pallas_call x0 -> x3, Pallas kernels: none -> 19.8 us  [the longest x1 6.98 us: second_core(): pl.pallas_call(second_core_kernel, out_shape=jax.ShapeDtypeStruct((n, lan...]
    all_to_all x4 -> x1, waiting for transfers between devices: 21 us -> 2.56 us  [exchange(): return lax.all_to_all(blocks, axes, split_axis=0, concat_axis=0, tiled=True)]
    all_to_all x3 -> x2, blocking collectives: 59.3 us -> 44.3 us  [exchange(): return lax.all_to_all(blocks, axes, split_axis=0, concat_axis=0, tiled=True)]
    all_to_all x4 -> x1, starting transfers between devices: 22.5 us -> 7.94 us  [exchange(): return lax.all_to_all(blocks, axes, split_axis=0, concat_axis=0, tiled=True)]
    dot_general x5 -> x0, matrix products: 10.3 us -> none  [the longest x2 5.24 us: orthonormal(): jnp.dot(sketch.T, sketch, precision=HIGH, preferred_element_type=jnp.floa...]
  transfers between devices with their start and end apart: 4 -> 17, of which waited for: 2 -> 10; matrix products, arithmetic and copies ran while one was open for 52% -> 0% of each run, Pallas kernels for 0% -> 0%
where the time goes in v2:
time: 163 us; the launch traced here: 162 us
  waiting for transfers between devices  58.2 us (36%)
  blocking collectives  44.3 us (27%)
  starting transfers between devices  30.2 us (19%)
  Pallas kernels  19.8 us (12%)
  matrix products  4.73 us (3%)
  local copies, waits for them, and re-layouts  2.56 us (2%)
  other arithmetic  1.95 us (1%)
    ppermute x16, waiting for transfers between devices, around(): lax.ppermute(block, axes, [(p, (p + step) % count) for p in range(count)])  55.6 us
    all_to_all x2, blocking collectives, exchange(): return lax.all_to_all(blocks, axes, split_axis=0, concat_axis=0, tiled=True)  44.3 us
    ppermute x16, starting transfers between devices, around(): lax.ppermute(block, axes, [(p, (p + step) % count) for p in range(count)])  22.3 us
    all_to_all x1, starting transfers between devices, exchange(): return lax.all_to_all(blocks, axes, split_axis=0, concat_axis=0, tiled=True)  7.94 us
    pallas_call x1, Pallas kernels, second_core(): pl.pallas_call(second_core_kernel, out_shape=jax.ShapeDtypeStruct((n, lan...  6.98 us
    pallas_call x1, Pallas kernels, project(): pl.pallas_call(project_kernel, out_shape=jax.ShapeDtypeStruct((rank // 2...  6.44 us
    pallas_call x1, Pallas kernels, first_basis(): pl.pallas_call(first_basis_kernel, out_shape=jax.ShapeDtypeStruct(sketch....  6.41 us
    dot_general x1, matrix products, on_device(): jnp.einsum('jik,kr->jir', tensor, omega_three, preferred_element_type=jnp...  4.73 us
  transfers between devices with their start and end apart: 17, of which 10 were waited for; matrix products, arithmetic and copies ran while one was open for 0% of the time, Pallas kernels for 0%

profile of v2, /device:TPU:0, one launch (start us, length us, event | category | flops | bytes accessed | tf_op | source)
XLA Modules:
  0.0 162.2 jit_solution(10742313908364539288)
XLA Ops:
  0.0 0.7 convert_bitcast_fusion
  0.7 0.8 bitcast_convert_fusion
  1.5 4.7 %multiply_reduce_fusion = f32[256,128]{0,1:T(8,128)S(1)} fusion(f32[256,64]{0,1:T(8,128)S(1)} %bitcast_convert_fusion, bf16[64,128,288]{1,2,0:T(8,128)(2,1)} %param.5, bf16[288,256]{1,0:T(8,128)(2,1)S(1)} %copy-done), kind=kOutput, calls=%fused_computation | convolution fusion | flops 1212121088 | bytes 5062656 | tf_op jit(solution)/shard_map/jik,kr->jir/dot_general | solution.py:240
  6.4 1.2 collective-permute-done
  7.7 1.7 %collective-permute-start.1 = (f32[64,256]{1,0:T(8,128)S(1)}, f32[64,256]{1,0:T(8,128)S(1)}, u32[]{:S(2)}, u32[]{:S(2)}) collective-permute-start(f32[64,256]{1,0:T(8,128)S(1)} %pad_maximum_fusion.4), channel_id=1, source_target_pairs={{0,2},{2,0},{1,3},{3,1},{4,6},{6,4},{5,7},{7,5},{8,10},{10,8},{9,1... | collective-permute-start | bytes 196616 | tf_op jit(solution)/shard_map/ppermute | solution.py:198
  9.5 2.6 %collective-permute-done.1 = f32[64,256]{1,0:T(8,128)S(1)} collective-permute-done((f32[64,256]{1,0:T(8,128)S(1)}, f32[64,256]{1,0:T(8,128)S(1)}, u32[]{:S(2)}, u32[]{:S(2)}) %collective-permute-start.1) | collective-permute-done | bytes 65568 | tf_op jit(solution)/shard_map/ppermute | solution.py:198
  12.2 1.6 %collective-permute-start.2 = (f32[72,256]{1,0:T(8,128)S(1)}, f32[72,256]{1,0:T(8,128)S(1)}, u32[]{:S(2)}, u32[]{:S(2)}) collective-permute-start(f32[72,256]{1,0:T(8,128)S(1)} %get-tuple-element.17), channel_id=1, source_target_pairs={{0,4},{4,8},{8,12},{12,0},{1,5},{5,9},{9,13},{13,1},{2,6},{6,10},{... | collective-permute-start | bytes 221192 | tf_op jit(solution)/shard_map/ppermute | solution.py:198
  13.8 2.7 %collective-permute-start.3 = (f32[72,256]{1,0:T(8,128)S(1)}, f32[72,256]{1,0:T(8,128)S(1)}, u32[]{:S(2)}, u32[]{:S(2)}) collective-permute-start(f32[72,256]{1,0:T(8,128)S(1)} %get-tuple-element.18), channel_id=1, source_target_pairs={{0,8},{4,12},{8,0},{12,4},{1,9},{5,13},{9,1},{13,5},{2,10},{6,14},... | collective-permute-start | bytes 221192 | tf_op jit(solution)/shard_map/ppermute | solution.py:198
  16.6 1.4 collective-permute-start.4
  18.0 7.9 %all-to-all-start = ((bf16[8,8,288,128]{3,2,1,0:T(8,128)(2,1)}), bf16[8,8,288,128]{3,2,1,0:T(8,128)(2,1)}, u32[]{:S(2)}, u32[]{:S(2)}) async-start(bf16[8,8,288,128]{3,2,1,0:T(8,128)(2,1)} %bitcast.123), calls=%async_computation | async-start | bytes 9437184 | tf_op jit(solution)/shard_map/all_to_all | solution.py:193
  26.0 0.7 collective-permute-start.7
  26.6 0.9 collective-permute-start.6
  27.5 1.9 %collective-permute-start.5 = (f32[8,256]{1,0:T(8,128)S(1)}, f32[8,256]{1,0:T(8,128)S(1)}, u32[]{:S(2)}, u32[]{:S(2)}) collective-permute-start(f32[8,256]{1,0:T(8,128)S(1)} %slice_add_fusion.2), channel_id=1, source_target_pairs={{0,12},{4,0},{8,4},{12,8},{1,13},{5,1},{9,5},{13,9},{2,14},{6,2},{... | collective-permute-start | bytes 24584 | tf_op jit(solution)/shard_map/ppermute | solution.py:198
  29.4 2.4 %collective-permute-done.5 = f32[8,256]{1,0:T(8,128)S(1)} collective-permute-done((f32[8,256]{1,0:T(8,128)S(1)}, f32[8,256]{1,0:T(8,128)S(1)}, u32[]{:S(2)}, u32[]{:S(2)}) %collective-permute-start.5) | collective-permute-done | bytes 8224 | tf_op jit(solution)/shard_map/ppermute | solution.py:198
  32.0 3.3 %collective-permute-start.8 = (f32[32,256]{1,0:T(8,128)S(1)}, f32[32,256]{1,0:T(8,128)S(1)}, u32[]{:S(2)}, u32[]{:S(2)}) collective-permute-start(f32[32,256]{1,0:T(8,128)S(1)} %dynamic-slice_bitcast_fusion.2), channel_id=1, source_target_pairs={{0,96},{32,0},{64,32},{96,64},{1,97},{33,1},{65,33},{97,65},{2,98}... | collective-permute-start | bytes 98312 | tf_op jit(solution)/shard_map/ppermute | solution.py:198
  35.3 2.3 %collective-permute-start.9 = (f32[32,256]{1,0:T(8,128)S(1)}, f32[32,256]{1,0:T(8,128)S(1)}, u32[]{:S(2)}, u32[]{:S(2)}) collective-permute-start(f32[32,256]{1,0:T(8,128)S(1)} %dynamic-slice_bitcast_fusion.2), channel_id=1, source_target_pairs={{0,64},{32,96},{64,0},{96,32},{1,65},{33,97},{65,1},{97,33},{2,66}... | collective-permute-start | bytes 98312 | tf_op jit(solution)/shard_map/ppermute | solution.py:198
  37.6 40.6 %collective-permute-done.8 = f32[32,256]{1,0:T(8,128)S(1)} collective-permute-done((f32[32,256]{1,0:T(8,128)S(1)}, f32[32,256]{1,0:T(8,128)S(1)}, u32[]{:S(2)}, u32[]{:S(2)}) %collective-permute-start.8) | collective-permute-done | bytes 32800 | tf_op jit(solution)/shard_map/ppermute | solution.py:198
  78.4 2.6 %all-to-all-done.moved_ref = bf16[8,8,288,128]{3,2,1,0:T(8,128)(2,1)} async-done(((bf16[8,8,288,128]{3,2,1,0:T(8,128)(2,1)}), bf16[8,8,288,128]{3,2,1,0:T(8,128)(2,1)}, u32[]{:S(2)}, u32[]{:S(2)}) %all-to-all-start) | async-done | bytes 4718624 | tf_op jit(solution)/shard_map/all_to_all | solution.py:193
  80.9 2.1 %collective-permute-start.11 = (f32[128,256]{1,0:T(8,128)S(1)}, f32[128,256]{1,0:T(8,128)S(1)}, u32[]{:S(2)}, u32[]{:S(2)}) collective-permute-start(f32[128,256]{1,0:T(8,128)S(1)} %bitcast.126), channel_id=1, source_target_pairs={{0,18},{2,0},{16,2},{18,16},{1,19},{3,1},{17,3},{19,17},{4,22},{6,... | collective-permute-start | bytes 393224 | tf_op jit(solution)/shard_map/ppermute | solution.py:198
  83.1 2.2 %collective-permute-start.12 = (f32[128,256]{1,0:T(8,128)S(1)}, f32[128,256]{1,0:T(8,128)S(1)}, u32[]{:S(2)}, u32[]{:S(2)}) collective-permute-start(f32[128,256]{1,0:T(8,128)S(1)} %bitcast.128), channel_id=1, source_target_pairs={{0,16},{2,18},{16,0},{18,2},{1,17},{3,19},{17,1},{19,3},{4,20},{6,... | collective-permute-start | bytes 393224 | tf_op jit(solution)/shard_map/ppermute | solution.py:198
  85.3 1.7 %collective-permute-done.11 = f32[128,256]{1,0:T(8,128)S(1)} collective-permute-done((f32[128,256]{1,0:T(8,128)S(1)}, f32[128,256]{1,0:T(8,128)S(1)}, u32[]{:S(2)}, u32[]{:S(2)}) %collective-permute-start.11) | collective-permute-done | bytes 131104 | tf_op jit(solution)/shard_map/ppermute | solution.py:198
  87.0 2.8 %collective-permute-done.12 = f32[128,256]{1,0:T(8,128)S(1)} collective-permute-done((f32[128,256]{1,0:T(8,128)S(1)}, f32[128,256]{1,0:T(8,128)S(1)}, u32[]{:S(2)}, u32[]{:S(2)}) %collective-permute-start.12) | collective-permute-done | bytes 131104 | tf_op jit(solution)/shard_map/ppermute | solution.py:198
  89.8 0.9 collective-permute-done.13
  91.2 1.8 %collective-permute-done.14 = f32[512,256]{1,0:T(8,128)S(1)} collective-permute-done((f32[512,256]{1,0:T(8,128)S(1)}, f32[512,256]{1,0:T(8,128)S(1)}, u32[]{:S(2)}, u32[]{:S(2)}) %collective-permute-start.14) | collective-permute-done | bytes 524320 | tf_op jit(solution)/shard_map/ppermute | solution.py:198
  93.2 6.4 %first_basis.1.basis_ref = bf16[256,1024]{1,0:T(8,128)(2,1)S(1)} custom-call(f32[1024,256]{1,0:T(8,128)S(1)} %bitcast.121), custom_call_target="tpu_custom_call" | custom-call | flops 4000000000 | bytes 2000000 | tf_op jit(solution)/shard_map/first_basis/pallas_call | solution.py:99
  99.6 6.4 %project.1 = bf16[1024,896]{1,0:T(8,128)(2,1)S(1)} custom-call(bf16[256,1024]{1,0:T(8,128)(2,1)S(1)} %first_basis.1.basis_ref, bf16[288,256]{1,0:T(8,128)(2,1)S(1)} %copy-done.1, f32[256,256]{1,0:T(8,128)S(1)} %bitcast.120, bf16[8,8,288,128]{3,2,1,0:T(8,128)(2,1)} %all-to-all-done.moved_ref), custom_call_target="tpu_custom_call" | custom-call | flops 2000000000 | bytes 8000000 | tf_op jit(solution)/shard_map/project/pallas_call | solution.py:180
  106.1 31.1 %all_to_all.15 = bf16[128,8,896]{2,1,0:T(8,128)(2,1)S(1)} all-to-all(bf16[128,8,896]{2,1,0:T(8,128)(2,1)S(1)} %bitcast.117), channel_id=1, replica_groups=mesh['z'=4,'yh'=2,'x'=4,'yl'=2,'c'=2] {'x','yl','c','z','yh'}, dimensions={0} | all-to-all | bytes 3670016 | tf_op jit(solution)/shard_map/all_to_all | solution.py:193
  137.2 1.0 collective-permute-start.15
  138.2 1.5 collective-permute-done.15.other_ref
  139.7 7.0 %second_core.1 = bf16[256,640]{1,0:T(8,128)(2,1)S(1)} custom-call(bf16[1024,896]{1,0:T(8,128)(2,1)S(1)} %bitcast.119, bf16[1024,256]{1,0:T(8,128)(2,1)S(1)} %collective-permute-done.15.other_ref), custom_call_target="tpu_custom_call" | custom-call | flops 4000000000 | bytes 3000000 | tf_op jit(solution)/shard_map/second_core/pallas_call | solution.py:121
  146.7 13.2 %all_to_all.16 = bf16[8,32,640]{2,1,0:T(8,128)(2,1)S(1)} all-to-all(bf16[8,32,640]{2,1,0:T(8,128)(2,1)S(1)} %bitcast.122), channel_id=1, replica_groups=mesh['z'=4,'yh'=2,'x'=4,'yl'=2,'c'=2] {'z','yh'}, dimensions={0} | all-to-all | bytes 655360 | tf_op jit(solution)/shard_map/all_to_all | solution.py:193
  160.8 1.4 reshape.59
  (70 shorter events, 2.0 us)
Async XLA Ops:
  0.0 1.5 copy-start
  6.3 1.4 collective-permute-start
  7.7 4.3 %collective-permute-start.1 = (f32[64,256]{1,0:T(8,128)S(1)}, f32[64,256]{1,0:T(8,128)S(1)}, u32[]{:S(2)}, u32[]{:S(2)}) collective-permute-start(f32[64,256]{1,0:T(8,128)S(1)} %pad_maximum_fusion.4), channel_id=1, source_target_pairs={{0,2},{2,0},{1,3},{3,1},{4,6},{6,4},{5,7},{7,5},{8,10},{10,8},{9,1... | collective-permute-start | bytes 196616 | tf_op jit(solution)/shard_map/ppermute | solution.py:198
  12.2 13.8 %collective-permute-start.2 = (f32[72,256]{1,0:T(8,128)S(1)}, f32[72,256]{1,0:T(8,128)S(1)}, u32[]{:S(2)}, u32[]{:S(2)}) collective-permute-start(f32[72,256]{1,0:T(8,128)S(1)} %get-tuple-element.17), channel_id=1, source_target_pairs={{0,4},{4,8},{8,12},{12,0},{1,5},{5,9},{9,13},{13,1},{2,6},{6,10},{... | collective-permute-start | bytes 221192 | tf_op jit(solution)/shard_map/ppermute | solution.py:198
  13.8 12.1 %collective-permute-start.3 = (f32[72,256]{1,0:T(8,128)S(1)}, f32[72,256]{1,0:T(8,128)S(1)}, u32[]{:S(2)}, u32[]{:S(2)}) collective-permute-start(f32[72,256]{1,0:T(8,128)S(1)} %get-tuple-element.18), channel_id=1, source_target_pairs={{0,8},{4,12},{8,0},{12,4},{1,9},{5,13},{9,1},{13,5},{2,10},{6,14},... | collective-permute-start | bytes 221192 | tf_op jit(solution)/shard_map/ppermute | solution.py:198
  16.6 9.4 %collective-permute-start.4 = (f32[72,256]{1,0:T(8,128)S(1)}, f32[72,256]{1,0:T(8,128)S(1)}, u32[]{:S(2)}, u32[]{:S(2)}) collective-permute-start(f32[72,256]{1,0:T(8,128)S(1)} %get-tuple-element.19), channel_id=1, source_target_pairs={{0,12},{4,0},{8,4},{12,8},{1,13},{5,1},{9,5},{13,9},{2,14},{6,2},{... | collective-permute-start | bytes 221192 | tf_op jit(solution)/shard_map/ppermute | solution.py:198
  18.0 62.9 %all-to-all-start = ((bf16[8,8,288,128]{3,2,1,0:T(8,128)(2,1)}), bf16[8,8,288,128]{3,2,1,0:T(8,128)(2,1)}, u32[]{:S(2)}, u32[]{:S(2)}) async-start(bf16[8,8,288,128]{3,2,1,0:T(8,128)(2,1)} %bitcast.123), calls=%async_computation | async-start | bytes 9437184 | tf_op jit(solution)/shard_map/all_to_all | solution.py:193
  26.0 5.9 %collective-permute-start.7 = (f32[8,256]{1,0:T(8,128)S(1)}, f32[8,256]{1,0:T(8,128)S(1)}, u32[]{:S(2)}, u32[]{:S(2)}) collective-permute-start(f32[8,256]{1,0:T(8,128)S(1)} %slice_add_fusion.2), channel_id=1, source_target_pairs={{0,4},{4,8},{8,12},{12,0},{1,5},{5,9},{9,13},{13,1},{2,6},{6,10},{... | collective-permute-start | bytes 24584 | tf_op jit(solution)/shard_map/ppermute | solution.py:198
  26.6 5.2 %collective-permute-start.6 = (f32[8,256]{1,0:T(8,128)S(1)}, f32[8,256]{1,0:T(8,128)S(1)}, u32[]{:S(2)}, u32[]{:S(2)}) collective-permute-start(f32[8,256]{1,0:T(8,128)S(1)} %slice_add_fusion.2), channel_id=1, source_target_pairs={{0,8},{4,12},{8,0},{12,4},{1,9},{5,13},{9,1},{13,5},{2,10},{6,14},... | collective-permute-start | bytes 24584 | tf_op jit(solution)/shard_map/ppermute | solution.py:198
  27.5 4.3 %collective-permute-start.5 = (f32[8,256]{1,0:T(8,128)S(1)}, f32[8,256]{1,0:T(8,128)S(1)}, u32[]{:S(2)}, u32[]{:S(2)}) collective-permute-start(f32[8,256]{1,0:T(8,128)S(1)} %slice_add_fusion.2), channel_id=1, source_target_pairs={{0,12},{4,0},{8,4},{12,8},{1,13},{5,1},{9,5},{13,9},{2,14},{6,2},{... | collective-permute-start | bytes 24584 | tf_op jit(solution)/shard_map/ppermute | solution.py:198
  32.0 46.3 %collective-permute-start.8 = (f32[32,256]{1,0:T(8,128)S(1)}, f32[32,256]{1,0:T(8,128)S(1)}, u32[]{:S(2)}, u32[]{:S(2)}) collective-permute-start(f32[32,256]{1,0:T(8,128)S(1)} %dynamic-slice_bitcast_fusion.2), channel_id=1, source_target_pairs={{0,96},{32,0},{64,32},{96,64},{1,97},{33,1},{65,33},{97,65},{2,98}... | collective-permute-start | bytes 98312 | tf_op jit(solution)/shard_map/ppermute | solution.py:198
  35.3 43.0 %collective-permute-start.10 = (f32[32,256]{1,0:T(8,128)S(1)}, f32[32,256]{1,0:T(8,128)S(1)}, u32[]{:S(2)}, u32[]{:S(2)}) collective-permute-start(f32[32,256]{1,0:T(8,128)S(1)} %dynamic-slice_bitcast_fusion.2), channel_id=1, source_target_pairs={{0,32},{32,64},{64,96},{96,0},{1,33},{33,65},{65,97},{97,1},{2,34}... | collective-permute-start | bytes 98312 | tf_op jit(solution)/shard_map/ppermute | solution.py:198
  35.3 43.0 %collective-permute-start.9 = (f32[32,256]{1,0:T(8,128)S(1)}, f32[32,256]{1,0:T(8,128)S(1)}, u32[]{:S(2)}, u32[]{:S(2)}) collective-permute-start(f32[32,256]{1,0:T(8,128)S(1)} %dynamic-slice_bitcast_fusion.2), channel_id=1, source_target_pairs={{0,64},{32,96},{64,0},{96,32},{1,65},{33,97},{65,1},{97,33},{2,66}... | collective-permute-start | bytes 98312 | tf_op jit(solution)/shard_map/ppermute | solution.py:198
  80.9 6.0 %collective-permute-start.11 = (f32[128,256]{1,0:T(8,128)S(1)}, f32[128,256]{1,0:T(8,128)S(1)}, u32[]{:S(2)}, u32[]{:S(2)}) collective-permute-start(f32[128,256]{1,0:T(8,128)S(1)} %bitcast.126), channel_id=1, source_target_pairs={{0,18},{2,0},{16,2},{18,16},{1,19},{3,1},{17,3},{19,17},{4,22},{6,... | collective-permute-start | bytes 393224 | tf_op jit(solution)/shard_map/ppermute | solution.py:198
  83.1 7.6 %collective-permute-start.13 = (f32[128,256]{1,0:T(8,128)S(1)}, f32[128,256]{1,0:T(8,128)S(1)}, u32[]{:S(2)}, u32[]{:S(2)}) collective-permute-start(f32[128,256]{1,0:T(8,128)S(1)} %bitcast.127), channel_id=1, source_target_pairs={{0,2},{2,16},{16,18},{18,0},{1,3},{3,17},{17,19},{19,1},{4,6},{6,2... | collective-permute-start | bytes 393224 | tf_op jit(solution)/shard_map/ppermute | solution.py:198
  83.1 6.7 %collective-permute-start.12 = (f32[128,256]{1,0:T(8,128)S(1)}, f32[128,256]{1,0:T(8,128)S(1)}, u32[]{:S(2)}, u32[]{:S(2)}) collective-permute-start(f32[128,256]{1,0:T(8,128)S(1)} %bitcast.128), channel_id=1, source_target_pairs={{0,16},{2,18},{16,0},{18,2},{1,17},{3,19},{17,1},{19,3},{4,20},{6,... | collective-permute-start | bytes 393224 | tf_op jit(solution)/shard_map/ppermute | solution.py:198
  90.8 2.2 %collective-permute-start.14 = (f32[512,256]{1,0:T(8,128)S(1)}, f32[512,256]{1,0:T(8,128)S(1)}, u32[]{:S(2)}, u32[]{:S(2)}) collective-permute-start(f32[512,256]{1,0:T(8,128)S(1)} %bitcast.124), channel_id=1, source_target_pairs={{0,1},{1,0},{2,3},{3,2},{4,5},{5,4},{6,7},{7,6},{8,9},{9,8},{10,11... | collective-permute-start | bytes 1572872 | tf_op jit(solution)/shard_map/ppermute | solution.py:198
  93.2 6.4 %copy-start.1 = (bf16[288,256]{1,0:T(8,128)(2,1)S(1)}, bf16[288,256]{1,0:T(8,128)(2,1)}, u32[]{:S(2)}) copy-start(bf16[288,256]{1,0:T(8,128)(2,1)} %plane_ref.1) | copy-start | bytes 442372
  137.2 2.5 %collective-permute-start.15 = (bf16[1024,256]{1,0:T(8,128)(2,1)S(1)}, bf16[1024,256]{1,0:T(8,128)(2,1)S(1)}, u32[]{:S(2)}, u32[]{:S(2)}) collective-permute-start(bf16[1024,256]{1,0:T(8,128)(2,1)S(1)} %slice.70), channel_id=1, source_target_pairs={{0,1},{1,0},{2,3},{3,2},{4,5},{5,4},{6,7},{7,6},{8,9},{9,8},{10,11... | collective-permute-start | bytes 1572872 | tf_op jit(solution)/shard_map/ppermute | solution.py:198

commit v3 on v2

v3 whole, which is shorter than its diff:
```python
import jax
import jax.numpy as jnp
from jax import lax
from jax.experimental import pallas as pl
from jax.experimental.pallas import tpu as pltpu
from jax.sharding import Mesh
from jax.sharding import PartitionSpec as P

HIGH = lax.Precision.HIGHEST


NT = (((1,), (1,)), ((), ()))
NN = (((1,), (0,)), ((), ()))
TN = (((0,), (0,)), ((), ()))


def mm(a, b, dims=NN, precision=None):
    return lax.dot_general(a, b, dims, precision=precision, preferred_element_type=jnp.float32)


def low(x):
    return x.astype(jnp.bfloat16)


def inverse_factor(s, basis_ref, a_ref, m_ref, turned):
    n = s.shape[1]
    row = lax.broadcasted_iota(jnp.int32, (n, n), 0)
    col = lax.broadcasted_iota(jnp.int32, (n, n), 1)
    eye = row == col
    one = jnp.where(eye, 1.0, 0.0)
    half = jnp.where(row > col, 1.0, 0.5 * one)

    def put(inverse):
        basis = mm(inverse, s, NT, HIGH) if turned else mm(s, inverse, NT, HIGH)
        basis_ref[...] = low(basis)

    gram = mm(s, s, TN, HIGH)
    on_diag = jnp.where(eye, gram, 0.0)
    inv_row = 0.9 * lax.rsqrt(jnp.sum(on_diag, axis=0, keepdims=True))
    inv_col = 0.9 * lax.rsqrt(jnp.sum(on_diag, axis=1, keepdims=True))
    scaled = gram * inv_col * inv_row

    h = scaled
    m = None
    early = 2
    for step in range(early):
        f = half * (h - one)
        fb = low(f)
        kb = low(one - f + half * mm(fb, fb, NT) + mm(fb, fb))
        m = kb if m is None else low(mm(kb, m))
        if step < early - 1:
            h = mm(low(mm(kb, low(h))), kb, NT)
    m = m.astype(jnp.float32)
    for _ in range(2):
        r = mm(mm(m, scaled, NN, HIGH), m, NT, HIGH) - one
        m = m - mm(half * r, m, NN, HIGH)
    good = jnp.logical_and(jnp.sum(r * r) < 1e-3, jnp.min(jnp.where(eye, m, 1.0)) > 0.0)
    put(m * inv_row)

    @pl.when(jnp.logical_not(good))
    def _():
        a_ref[...] = scaled
        m_ref[...] = one

        def step(j, carry):
            a = a_ref[...]
            pivot_row = a_ref[pl.ds(j, 1), :]
            unit_row = m_ref[pl.ds(j, 1), :]
            column = jnp.sum(jnp.where(col == j, a, 0.0), axis=1, keepdims=True)
            pivot = jnp.sum(jnp.where(col[:1] == j, pivot_row, 0.0), axis=1, keepdims=True)
            f = jnp.where(row[:, :1] > j, column / pivot, 0.0)
            a_ref[...] = a - f * pivot_row
            m_ref[...] = m_ref[...] - f * unit_row
            return carry

        lax.fori_loop(0, n, step, 0)
        pivots = jnp.sum(jnp.where(eye, a_ref[...], 0.0), axis=1, keepdims=True)
        direct = m_ref[...] * lax.rsqrt(pivots) * inv_row
        put(direct)


VMEM = pl.BlockSpec(memory_space=pltpu.VMEM)
PARAMS = pltpu.CompilerParams(vmem_limit_bytes=32 * 1024 * 1024)
ROOMY = pltpu.CompilerParams(vmem_limit_bytes=60 * 1024 * 1024)


def cost(flops, size):
    return pl.CostEstimate(flops=flops, bytes_accessed=size, transcendentals=0)


def first_basis_kernel(s_ref, basis_ref, a_ref, m_ref):
    places = [
        ((c * 4 + z) * 2 + yh) * 2 + yl
        for z in range(4)
        for yh in range(2)
        for yl in range(2)
        for c in range(2)
    ]
    s = jnp.concatenate([s_ref[place * 32 : place * 32 + 32] for place in places], axis=0)
    inverse_factor(s, basis_ref, a_ref, m_ref, False)


def first_basis(sketch):
    n = sketch.shape[1]
    return pl.pallas_call(
        first_basis_kernel,
        out_shape=jax.ShapeDtypeStruct(sketch.shape, jnp.bfloat16),
        in_specs=[VMEM],
        out_specs=VMEM,
        scratch_shapes=[pltpu.VMEM((n, n), jnp.float32)] * 2,
        compiler_params=PARAMS,
        cost_estimate=cost(0, 0),
        name="first_basis",
    )(sketch)


def second_core_kernel(got_ref, other_ref, core_ref, basis_ref, a_ref, m_ref):
    lanes = core_ref.shape[1]
    sketch = got_ref[:, lanes:].astype(jnp.float32) + other_ref[...].astype(jnp.float32)
    inverse_factor(sketch, basis_ref, a_ref, m_ref, True)
    core_ref[...] = mm(basis_ref[...], got_ref[:, :lanes]).astype(core_ref.dtype)


def second_core(got, other):
    n = other.shape[1]
    lanes = got.shape[1] - n
    return pl.pallas_call(
        second_core_kernel,
        out_shape=jax.ShapeDtypeStruct((n, lanes), jnp.bfloat16),
        in_specs=[VMEM] * 2,
        out_specs=VMEM,
        scratch_shapes=[pltpu.VMEM((n, got.shape[0]), jnp.bfloat16)]
        + [pltpu.VMEM((n, n), jnp.float32)] * 2,
        compiler_params=PARAMS,
        cost_estimate=cost(4 * 10**9, 3 * 10**6),
        name="second_core",
    )(got, other)


def first_sums_kernel(two_ref, three_ref, slabs_ref, out_ref):
    step = pl.program_id(0)
    count = slabs_ref.shape[0]
    weight = two_ref[pl.ds(pl.multiple_of(step * count, count), count), :]
    weight = weight.astype(jnp.float32)
    total = None
    for j in range(count):
        inner = mm(slabs_ref[j], three_ref[...], TN)
        term = inner * weight[j : j + 1]
        total = term if total is None else total + term

    @pl.when(step == 0)
    def _():
        out_ref[...] = total

    @pl.when(step > 0)
    def _():
        out_ref[...] += total


def first_sums(tensor, omega_two, omega_three):
    rows, cols, planes = tensor.shape
    rank = omega_two.shape[1]
    count = 16
    return pl.pallas_call(
        first_sums_kernel,
        grid=(rows // count,),
        out_shape=jax.ShapeDtypeStruct((cols, rank), jnp.float32),
        in_specs=[
            pl.BlockSpec((rows, rank), lambda step: (0, 0)),
            pl.BlockSpec((planes, rank), lambda step: (0, 0)),
            pl.BlockSpec((count, planes, cols), lambda step: (step, 0, 0)),
        ],
        out_specs=pl.BlockSpec((cols, rank), lambda step: (0, 0)),
        compiler_params=ROOMY,
        cost_estimate=cost(10**9, 5 * 10**6),
        name="first_sums",
    )(omega_two, omega_three, jnp.swapaxes(tensor, 1, 2))


def project_kernel(basis_ref, plane_ref, rank_ref, moved_ref, split_ref, core_ref, slab_ref, sems):
    rows, rank, planes = core_ref.shape
    loads = [
        pltpu.make_async_copy(moved_ref.at[:, j], slab_ref.at[j], sems.at[j]) for j in range(rows)
    ]
    for load in loads:
        load.start()
    basis = basis_ref[...]
    weight = plane_ref[...].astype(jnp.float32)
    sketch = []
    for j in range(rows):
        loads[j].wait()
        slab = jnp.concatenate([slab_ref[j, b] for b in range(slab_ref.shape[1])], axis=1)
        core = mm(slab, basis)
        core_ref[j] = low(core.T)
        inner = mm(low(core), rank_ref[...])
        sketch.append(jnp.sum(inner * weight, axis=0, keepdims=True))
    sketch = jnp.concatenate(sketch, axis=0)
    upper = low(sketch)
    lower = low(sketch - upper.astype(jnp.float32))
    copies = 64 // rows
    halves = jnp.concatenate([upper] * copies + [lower] * copies, axis=0)

    group = 256 // rows
    pairs = group // 2
    target = lax.broadcasted_iota(jnp.int32, (256, 256), 0)
    source = lax.broadcasted_iota(jnp.int32, (256, 256), 1)
    wanted = (target % rows) * group + 2 * ((target // rows) % pairs) + target // (rows * pairs)
    permute = low(jnp.where(source == wanted, 1.0, 0.0))
    full = planes // 128 * 128
    gap = jnp.zeros((128, 128 - 2 * (planes - full)), jnp.bfloat16)
    for g in range(rank // group):
        mixed = [core_ref[j, g * group : (g + 1) * group] for j in range(rows)]
        sorted_rows = low(mm(permute, jnp.concatenate(mixed, axis=0)))
        even, odd = sorted_rows[:128], sorted_rows[128:]
        split_ref[g * 128 : (g + 1) * 128] = jnp.concatenate(
            [even[:, :full], odd[:, :full], even[:, full:], odd[:, full:], gap, halves], axis=1
        )


def project(basis, sketch_plane, sketch_rank, moved):
    blocks, rows, planes, width = moved.shape
    rank = basis.shape[1]
    lanes = 2 * (planes // 128) * 128 + 128
    return pl.pallas_call(
        project_kernel,
        out_shape=jax.ShapeDtypeStruct((rank // 2 * rows, lanes + rank), jnp.bfloat16),
        in_specs=[VMEM] * 3 + [pl.BlockSpec(memory_space=pl.ANY)],
        out_specs=VMEM,
        scratch_shapes=[
            pltpu.VMEM((rows, rank, planes), jnp.bfloat16),
            pltpu.VMEM((rows, blocks, planes, width), jnp.bfloat16),
            pltpu.SemaphoreType.DMA((rows,)),
        ],
        compiler_params=PARAMS,
        cost_estimate=cost(2 * 10**9, 8 * 10**6),
        name="project",
    )(basis, sketch_plane, sketch_rank, moved)


def merge_kernel(got_ref, out_ref):
    blocks, count, _ = got_ref.shape
    planes = out_ref.shape[2]
    full = planes // 128 * 128
    rest = planes - full
    group = 256 // (2 * blocks)
    target = lax.broadcasted_iota(jnp.int32, (256, 256), 0)
    source = lax.broadcasted_iota(jnp.int32, (256, 256), 1)
    wanted = (target % (2 * blocks)) * group + target // (2 * blocks)
    permute = low(jnp.where(source == wanted, 1.0, 0.0))
    for g in range(count // group):
        rows = []
        for b in range(blocks):
            got = got_ref[b, g * group : (g + 1) * group]
            tail = 2 * full
            rows.append(jnp.concatenate([got[:, :full], got[:, tail : tail + rest]], axis=1))
            rows.append(
                jnp.concatenate([got[:, full:tail], got[:, tail + rest : tail + 2 * rest]], axis=1)
            )
        moved = mm(permute, jnp.concatenate(rows, axis=0))
        out_ref[g * group : (g + 1) * group] = moved.reshape(group, 2 * blocks, planes)


def merge(got, planes):
    return pl.pallas_call(
        merge_kernel,
        out_shape=jax.ShapeDtypeStruct((got.shape[1], 2 * got.shape[0], planes), jnp.float32),
        in_specs=[VMEM],
        out_specs=VMEM,
        compiler_params=PARAMS,
        cost_estimate=cost(10**8, 10**6),
        name="merge",
    )(got)


def exchange(blocks, axes):
    return lax.all_to_all(blocks, axes, split_axis=0, concat_axis=0, tiled=True)


def gather(rows, axes, count):
    shared = jnp.broadcast_to(rows[None], (count,) + rows.shape)
    return exchange(shared, axes).reshape(count * rows.shape[0], rows.shape[1])


def around(block, axes, step):
    count = lax.axis_size(axes)
    return lax.ppermute(block, axes, [(p, (p + step) % count) for p in range(count)])


def ordered(blocks, place):
    count = len(blocks)
    turned = jnp.stack(blocks[::-1] * 2)
    return lax.dynamic_slice_in_dim(turned, count - 1 - place, count, 0)


def collect(block, axes):
    count = lax.axis_size(axes)
    blocks = [block] + [around(block, axes, step) for step in range(1, count)]
    every = ordered(blocks, lax.axis_index(axes))
    return every.reshape((-1,) + block.shape[1:])


AF = ("z", "yh")
SA = ("x", "yl", "c")


def on_device(tensor, omega_two, omega_three, sketch_rank, sketch_plane):
    n_af = lax.axis_size(AF)
    n_sa = lax.axis_size(SA)
    n_all = n_af * n_sa
    local_rows, local_cols, planes = tensor.shape
    rank = omega_two.shape[1]
    fine_rows = local_rows // n_af

    rows = first_sums(tensor, omega_two, omega_three)
    some_rank = collect(sketch_rank, "yl")

    parts = exchange(rows.reshape(4, -1, rank), ("yl", "c"))
    rows, some_rank = lax.optimization_barrier((jnp.sum(parts, axis=0), some_rank))
    rows = gather(rows, AF + ("yl",), n_af * 2)

    rows, tensor = lax.optimization_barrier((rows, tensor))
    pieces = jnp.swapaxes(tensor, 1, 2).reshape(n_af, fine_rows, planes, local_cols)
    moved = exchange(pieces, AF)

    n_x, at = lax.axis_size("x"), lax.axis_index("x")
    shares = rows.reshape(n_x, -1, rank)
    rows = lax.dynamic_index_in_dim(shares, at, 0, keepdims=False)
    for step in range(1, n_x):
        share = lax.dynamic_index_in_dim(shares, (at + step) % n_x, 0, keepdims=False)
        rows = rows + around(share, "x", step)
    rows = collect(collect(rows, "x"), "c")
    whole_rank = collect(collect(some_rank, "c"), "x").reshape(4, 2, 2, -1, rank)
    whole_rank = whole_rank.swapaxes(1, 2).reshape(rank, rank)
    basis_low = first_basis(rows)

    split = project(basis_low, sketch_plane, whole_rank, moved)
    got = exchange(split.reshape(n_all, fine_rows, -1), SA + AF).reshape(n_all * fine_rows, -1)
    core = second_core(got, around(got[:, -rank:], "c", 1))

    return merge(exchange(core.reshape(n_af, rank // n_af, -1), AF), planes)


def solution(mesh):
    grid = Mesh(mesh.devices.reshape(4, 2, 4, 2, 2), ("z", "yh", "x", "yl", "c"))
    placed = (P(SA, AF, None), P(SA, None), P(), P(SA, None), P())
    return jax.shard_map(
        on_device, mesh=grid, in_specs=placed, out_specs=P(AF, SA, None), check_vma=False
    )
```

time: 163 us -> 158 us (0.969)
  Pallas kernels: 19.8 us -> 27.3 us
  waiting for transfers between devices: 58.2 us -> 50.8 us
  matrix products: 4.73 us -> 0 us
  starting transfers between devices: 30.2 us -> 32.3 us
    ppermute x16 -> x13, waiting for transfers between devices: 55.6 us -> 14.8 us  [around(): lax.ppermute(block, axes, [(p, (p + step) % count) for p in range(count)])]
    all_to_all x1 -> x3, waiting for transfers between devices: 2.56 us -> 36 us  [exchange(): return lax.all_to_all(blocks, axes, split_axis=0, concat_axis=0, tiled=True)]
    all_to_all x1 -> x3, starting transfers between devices: 7.94 us -> 15.7 us  [exchange(): return lax.all_to_all(blocks, axes, split_axis=0, concat_axis=0, tiled=True)]
    pallas_call x0 -> x2, Pallas kernels: none -> 6.88 us  [the longest x1 5.66 us: first_sums(): pl.pallas_call(first_sums_kernel, grid=(rows // count,), out_shape=jax.Sh...]
    ppermute x16 -> x13, starting transfers between devices: 22.3 us -> 16.6 us  [around(): lax.ppermute(block, axes, [(p, (p + step) % count) for p in range(count)])]
    dot_general x1 -> x0, matrix products: 4.73 us -> none  [on_device(): jnp.einsum('jik,kr->jir', tensor, omega_three, preferred_element_type=jnp...]
  transfers between devices with their start and end apart: 17 -> 16, of which waited for: 10 -> 12; matrix products, arithmetic and copies ran while one was open for 0% -> 0% of each run, Pallas kernels for 0% -> 8%
where the time goes in v3:
time: 158 us
  waiting for transfers between devices  50.8 us (32%)
  blocking collectives  45.5 us (29%)
  starting transfers between devices  32.3 us (20%)
  Pallas kernels  27.3 us (17%)
    all_to_all x2, blocking collectives, exchange(): return lax.all_to_all(blocks, axes, split_axis=0, concat_axis=0, tiled=True)  45.5 us
    all_to_all x3, waiting for transfers between devices, exchange(): return lax.all_to_all(blocks, axes, split_axis=0, concat_axis=0, tiled=True)  36 us
    ppermute x13, starting transfers between devices, around(): lax.ppermute(block, axes, [(p, (p + step) % count) for p in range(count)])  16.6 us
    all_to_all x3, starting transfers between devices, exchange(): return lax.all_to_all(blocks, axes, split_axis=0, concat_axis=0, tiled=True)  15.7 us
    ppermute x13, waiting for transfers between devices, around(): lax.ppermute(block, axes, [(p, (p + step) % count) for p in range(count)])  14.8 us
    pallas_call x1, Pallas kernels, second_core(): pl.pallas_call(second_core_kernel, out_shape=jax.ShapeDtypeStruct((n, lan...  6.98 us
    pallas_call x1, Pallas kernels, first_basis(): pl.pallas_call(first_basis_kernel, out_shape=jax.ShapeDtypeStruct(sketch....  6.9 us
    pallas_call x1, Pallas kernels, project(): pl.pallas_call(project_kernel, out_shape=jax.ShapeDtypeStruct((rank // 2...  6.54 us
  transfers between devices with their start and end apart: 16, of which 12 were waited for; matrix products, arithmetic and copies ran while one was open for 0% of the time, Pallas kernels for 8%

profile of v3, /device:TPU:0, one launch (start us, length us, event | category | flops | bytes accessed | tf_op | source)
XLA Modules:
  0.0 157.6 jit_solution(1491609037038810965)
XLA Ops:
  0.0 1.7 %collective-permute-start = (bf16[16,256]{1,0:T(8,128)(2,1)}, bf16[16,256]{1,0:T(8,128)(2,1)S(1)}, u32[]{:S(2)}, u32[]{:S(2)}) collective-permute-start(bf16[16,256]{1,0:T(8,128)(2,1)} %param.8), channel_id=1, source_target_pairs={{0,2},{2,0},{1,3},{3,1},{4,6},{6,4},{5,7},{7,5},{8,10},{10,8},{9,1... | collective-permute-start | bytes 24584 | tf_op jit(solution)/shard_map/ppermute | solution.py:286
  1.7 5.7 %first_sums.1 = f32[128,256]{1,0:T(8,128)} custom-call(bf16[64,256]{1,0:T(8,128)(2,1)} %two_ref.1, bf16[288,256]{1,0:T(8,128)(2,1)} %three_ref.1, bf16[64,288,128]{2,1,0:T(8,128)(2,1)} %bitcast.68), custom_call_target="tpu_custom_call" | custom-call | flops 1000000000 | bytes 5000000 | tf_op jit(solution)/shard_map/first_sums/pallas_call | solution.py:164
  7.3 3.3 %all-to-all-start = ((f32[4,32,256]{2,1,0:T(8,128)}), f32[4,32,256]{2,1,0:T(8,128)S(1)}, u32[]{:S(2)}, u32[]{:S(2)}) async-start(f32[4,32,256]{2,1,0:T(8,128)} %bitcast.75), calls=%async_computation | async-start | bytes 262144 | tf_op jit(solution)/shard_map/all_to_all | solution.py:276
  10.7 4.5 %all-to-all-done = f32[4,32,256]{2,1,0:T(8,128)S(1)} async-done(((f32[4,32,256]{2,1,0:T(8,128)}), f32[4,32,256]{2,1,0:T(8,128)S(1)}, u32[]{:S(2)}, u32[]{:S(2)}) %all-to-all-start) | async-done | bytes 131104 | tf_op jit(solution)/shard_map/all_to_all | solution.py:276
  15.3 0.8 broadcast_in_dim.2
  16.1 7.7 %all-to-all-start.1 = ((f32[16,32,256]{2,1,0:T(8,128)}), f32[16,32,256]{2,1,0:T(8,128)S(1)}, u32[]{:S(2)}, u32[]{:S(2)}) async-start(f32[16,32,256]{2,1,0:T(8,128)} %broadcast_in_dim.2), calls=%async_computation.1 | async-start | bytes 1048576 | tf_op jit(solution)/shard_map/all_to_all | solution.py:276
  24.0 1.2 collective-permute-done.8
  25.2 2.8 %collective-permute-start.9 = (bf16[64,256]{1,0:T(8,128)(2,1)S(1)}, bf16[64,256]{1,0:T(8,128)(2,1)S(1)}, u32[]{:S(2)}, u32[]{:S(2)}) collective-permute-start(bf16[64,256]{1,0:T(8,128)(2,1)S(1)} %bitcast.77), channel_id=1, source_target_pairs={{0,12},{4,0},{8,4},{12,8},{1,13},{5,1},{9,5},{13,9},{2,14},{6,2},{... | collective-permute-start | bytes 98312 | tf_op jit(solution)/shard_map/ppermute | solution.py:286
  28.0 0.8 collective-permute-start.10
  28.8 0.9 collective-permute-start.11
  29.7 5.4 %all-to-all-done.1 = f32[16,32,256]{2,1,0:T(8,128)S(1)} async-done(((f32[16,32,256]{2,1,0:T(8,128)}), f32[16,32,256]{2,1,0:T(8,128)S(1)}, u32[]{:S(2)}, u32[]{:S(2)}) %all-to-all-start.1) | async-done | bytes 524320 | tf_op jit(solution)/shard_map/all_to_all | solution.py:276
  35.0 4.6 %all-to-all-start.2 = ((bf16[8,8,288,128]{3,2,1,0:T(8,128)(2,1)}), bf16[8,8,288,128]{3,2,1,0:T(8,128)(2,1)}, u32[]{:S(2)}, u32[]{:S(2)}) async-start(bf16[8,8,288,128]{3,2,1,0:T(8,128)(2,1)} %bitcast.69), calls=%async_computation.2 | async-start | bytes 9437184 | tf_op jit(solution)/shard_map/all_to_all | solution.py:276
  39.7 1.6 collective-permute-start.1
  41.3 2.7 %collective-permute-start.2 = (f32[128,256]{1,0:T(8,128)S(1)}, f32[128,256]{1,0:T(8,128)S(1)}, u32[]{:S(2)}, u32[]{:S(2)}) collective-permute-start(f32[128,256]{1,0:T(8,128)S(1)} %get-tuple-element.15), channel_id=1, source_target_pairs={{0,8},{4,12},{8,0},{12,4},{1,9},{5,13},{9,1},{13,5},{2,10},{6,14},... | collective-permute-start | bytes 393224 | tf_op jit(solution)/shard_map/ppermute | solution.py:286
  44.0 1.4 collective-permute-start.3
  45.5 1.6 %collective-permute-done.1 = f32[128,256]{1,0:T(8,128)S(1)} collective-permute-done((f32[128,256]{1,0:T(8,128)S(1)}, f32[128,256]{1,0:T(8,128)S(1)}, u32[]{:S(2)}, u32[]{:S(2)}) %collective-permute-start.1) | collective-permute-done | bytes 131104 | tf_op jit(solution)/shard_map/ppermute | solution.py:286
  47.1 1.4 collective-permute-done.2
  49.0 2.7 %collective-permute-start.4 = (f32[128,256]{1,0:T(8,128)S(1)}, f32[128,256]{1,0:T(8,128)S(1)}, u32[]{:S(2)}, u32[]{:S(2)}) collective-permute-start(f32[128,256]{1,0:T(8,128)S(1)} %fusion.4), channel_id=1, source_target_pairs={{0,12},{4,0},{8,4},{12,8},{1,13},{5,1},{9,5},{13,9},{2,14},{6,2},{... | collective-permute-start | bytes 393224 | tf_op jit(solution)/shard_map/ppermute | solution.py:286
  51.8 0.9 collective-permute-start.5
  52.9 2.8 %collective-permute-done.4 = f32[128,256]{1,0:T(8,128)S(1)} collective-permute-done((f32[128,256]{1,0:T(8,128)S(1)}, f32[128,256]{1,0:T(8,128)S(1)}, u32[]{:S(2)}, u32[]{:S(2)}) %collective-permute-start.4) | collective-permute-done | bytes 131104 | tf_op jit(solution)/shard_map/ppermute | solution.py:286
  55.7 2.6 %collective-permute-done.5 = f32[128,256]{1,0:T(8,128)S(1)} collective-permute-done((f32[128,256]{1,0:T(8,128)S(1)}, f32[128,256]{1,0:T(8,128)S(1)}, u32[]{:S(2)}, u32[]{:S(2)}) %collective-permute-start.5) | collective-permute-done | bytes 131104 | tf_op jit(solution)/shard_map/ppermute | solution.py:286
  58.3 1.3 collective-permute-done.6
  60.0 1.8 %collective-permute-done.7 = f32[512,256]{1,0:T(8,128)S(1)} collective-permute-done((f32[512,256]{1,0:T(8,128)S(1)}, f32[512,256]{1,0:T(8,128)S(1)}, u32[]{:S(2)}, u32[]{:S(2)}) %collective-permute-start.7) | collective-permute-done | bytes 524320 | tf_op jit(solution)/shard_map/ppermute | solution.py:286
  62.0 6.9 %first_basis.1.basis_ref = bf16[1024,256]{1,0:T(8,128)(2,1)S(1)} custom-call(f32[1024,256]{1,0:T(8,128)S(1)} %bitcast.62), custom_call_target="tpu_custom_call" | custom-call | tf_op jit(solution)/shard_map/first_basis/pallas_call | solution.py:105
  68.9 26.1 %all-to-all-done.2.moved_ref = bf16[8,8,288,128]{3,2,1,0:T(8,128)(2,1)} async-done(((bf16[8,8,288,128]{3,2,1,0:T(8,128)(2,1)}), bf16[8,8,288,128]{3,2,1,0:T(8,128)(2,1)}, u32[]{:S(2)}, u32[]{:S(2)}) %all-to-all-start.2) | async-done | bytes 4718624 | tf_op jit(solution)/shard_map/all_to_all | solution.py:276
  95.0 6.5 %project.1 = bf16[1024,896]{1,0:T(8,128)(2,1)S(1)} custom-call(bf16[1024,256]{1,0:T(8,128)(2,1)S(1)} %first_basis.1.basis_ref, bf16[288,256]{1,0:T(8,128)(2,1)S(1)} %copy-done, bf16[256,256]{1,0:T(8,128)(2,1)S(1)} %bitcast.67, bf16[8,8,288,128]{3,2,1,0:T(8,128)(2,1)} %all-to-all-done.2.moved_ref), custom_call_target="tpu_custom_call" | custom-call | flops 2000000000 | bytes 8000000 | tf_op jit(solution)/shard_map/project/pallas_call | solution.py:224
  101.5 32.3 %all_to_all.25 = bf16[128,8,896]{2,1,0:T(8,128)(2,1)S(1)} all-to-all(bf16[128,8,896]{2,1,0:T(8,128)(2,1)S(1)} %bitcast.65), channel_id=1, replica_groups=mesh['z'=4,'yh'=2,'x'=4,'yl'=2,'c'=2] {'x','yl','c','z','yh'}, dimensions={0} | all-to-all | bytes 3670016 | tf_op jit(solution)/shard_map/all_to_all | solution.py:276
  133.8 0.8 collective-permute-start.12
  134.6 1.5 collective-permute-done.12.other_ref
  136.1 7.0 %second_core.1 = bf16[256,640]{1,0:T(8,128)(2,1)S(1)} custom-call(bf16[1024,896]{1,0:T(8,128)(2,1)S(1)} %bitcast.64, bf16[1024,256]{1,0:T(8,128)(2,1)S(1)} %collective-permute-done.12.other_ref), custom_call_target="tpu_custom_call" | custom-call | flops 4000000000 | bytes 3000000 | tf_op jit(solution)/shard_map/second_core/pallas_call | solution.py:127
  143.1 13.2 %all_to_all.26.got_ref = bf16[8,32,640]{2,1,0:T(8,128)(2,1)S(1)} all-to-all(bf16[8,32,640]{2,1,0:T(8,128)(2,1)S(1)} %bitcast.66), channel_id=1, replica_groups=mesh['z'=4,'yh'=2,'x'=4,'yl'=2,'c'=2] {'z','yh'}, dimensions={0} | all-to-all | bytes 655360 | tf_op jit(solution)/shard_map/all_to_all | solution.py:276
  156.3 1.2 merge.1
  (38 shorter events, 1.4 us)
Async XLA Ops:
  0.0 10.7 %collective-permute-start = (bf16[16,256]{1,0:T(8,128)(2,1)}, bf16[16,256]{1,0:T(8,128)(2,1)S(1)}, u32[]{:S(2)}, u32[]{:S(2)}) collective-permute-start(bf16[16,256]{1,0:T(8,128)(2,1)} %param.8), channel_id=1, source_target_pairs={{0,2},{2,0},{1,3},{3,1},{4,6},{6,4},{5,7},{7,5},{8,10},{10,8},{9,1... | collective-permute-start | bytes 24584 | tf_op jit(solution)/shard_map/ppermute | solution.py:286
  1.7 9.0 %copy-start.1 = (bf16[16,256]{1,0:T(8,128)(2,1)S(1)}, bf16[16,256]{1,0:T(8,128)(2,1)}, u32[]{:S(2)}) copy-start(bf16[16,256]{1,0:T(8,128)(2,1)} %param.8) | copy-start | bytes 24580
  7.3 7.9 %all-to-all-start = ((f32[4,32,256]{2,1,0:T(8,128)}), f32[4,32,256]{2,1,0:T(8,128)S(1)}, u32[]{:S(2)}, u32[]{:S(2)}) async-start(f32[4,32,256]{2,1,0:T(8,128)} %bitcast.75), calls=%async_computation | async-start | bytes 262144 | tf_op jit(solution)/shard_map/all_to_all | solution.py:276
  16.1 18.9 %all-to-all-start.1 = ((f32[16,32,256]{2,1,0:T(8,128)}), f32[16,32,256]{2,1,0:T(8,128)S(1)}, u32[]{:S(2)}, u32[]{:S(2)}) async-start(f32[16,32,256]{2,1,0:T(8,128)} %broadcast_in_dim.2), calls=%async_computation.1 | async-start | bytes 1048576 | tf_op jit(solution)/shard_map/all_to_all | solution.py:276
  23.9 1.3 collective-permute-start.8
  25.2 14.5 %collective-permute-start.9 = (bf16[64,256]{1,0:T(8,128)(2,1)S(1)}, bf16[64,256]{1,0:T(8,128)(2,1)S(1)}, u32[]{:S(2)}, u32[]{:S(2)}) collective-permute-start(bf16[64,256]{1,0:T(8,128)(2,1)S(1)} %bitcast.77), channel_id=1, source_target_pairs={{0,12},{4,0},{8,4},{12,8},{1,13},{5,1},{9,5},{13,9},{2,14},{6,2},{... | collective-permute-start | bytes 98312 | tf_op jit(solution)/shard_map/ppermute | solution.py:286
  28.0 11.7 %collective-permute-start.10 = (bf16[64,256]{1,0:T(8,128)(2,1)S(1)}, bf16[64,256]{1,0:T(8,128)(2,1)S(1)}, u32[]{:S(2)}, u32[]{:S(2)}) collective-permute-start(bf16[64,256]{1,0:T(8,128)(2,1)S(1)} %bitcast.78), channel_id=1, source_target_pairs={{0,8},{4,12},{8,0},{12,4},{1,9},{5,13},{9,1},{13,5},{2,10},{6,14},... | collective-permute-start | bytes 98312 | tf_op jit(solution)/shard_map/ppermute | solution.py:286
  28.8 16.7 %collective-permute-start.11 = (bf16[64,256]{1,0:T(8,128)(2,1)S(1)}, bf16[64,256]{1,0:T(8,128)(2,1)S(1)}, u32[]{:S(2)}, u32[]{:S(2)}) collective-permute-start(bf16[64,256]{1,0:T(8,128)(2,1)S(1)} %bitcast.79), channel_id=1, source_target_pairs={{0,4},{4,8},{8,12},{12,0},{1,5},{5,9},{9,13},{13,1},{2,6},{6,10},{... | collective-permute-start | bytes 98312 | tf_op jit(solution)/shard_map/ppermute | solution.py:286
  35.0 60.0 %all-to-all-start.2 = ((bf16[8,8,288,128]{3,2,1,0:T(8,128)(2,1)}), bf16[8,8,288,128]{3,2,1,0:T(8,128)(2,1)}, u32[]{:S(2)}, u32[]{:S(2)}) async-start(bf16[8,8,288,128]{3,2,1,0:T(8,128)(2,1)} %bitcast.69), calls=%async_computation.2 | async-start | bytes 9437184 | tf_op jit(solution)/shard_map/all_to_all | solution.py:276
  39.7 7.4 %collective-permute-start.1 = (f32[128,256]{1,0:T(8,128)S(1)}, f32[128,256]{1,0:T(8,128)S(1)}, u32[]{:S(2)}, u32[]{:S(2)}) collective-permute-start(f32[128,256]{1,0:T(8,128)S(1)} %get-tuple-element.13), channel_id=1, source_target_pairs={{0,4},{4,8},{8,12},{12,0},{1,5},{5,9},{9,13},{13,1},{2,6},{6,10},{... | collective-permute-start | bytes 393224 | tf_op jit(solution)/shard_map/ppermute | solution.py:286
  41.3 7.2 %collective-permute-start.2 = (f32[128,256]{1,0:T(8,128)S(1)}, f32[128,256]{1,0:T(8,128)S(1)}, u32[]{:S(2)}, u32[]{:S(2)}) collective-permute-start(f32[128,256]{1,0:T(8,128)S(1)} %get-tuple-element.15), channel_id=1, source_target_pairs={{0,8},{4,12},{8,0},{12,4},{1,9},{5,13},{9,1},{13,5},{2,10},{6,14},... | collective-permute-start | bytes 393224 | tf_op jit(solution)/shard_map/ppermute | solution.py:286
  44.0 5.0 %collective-permute-start.3 = (f32[128,256]{1,0:T(8,128)S(1)}, f32[128,256]{1,0:T(8,128)S(1)}, u32[]{:S(2)}, u32[]{:S(2)}) collective-permute-start(f32[128,256]{1,0:T(8,128)S(1)} %get-tuple-element.14), channel_id=1, source_target_pairs={{0,12},{4,0},{8,4},{12,8},{1,13},{5,1},{9,5},{13,9},{2,14},{6,2},{... | collective-permute-start | bytes 393224 | tf_op jit(solution)/shard_map/ppermute | solution.py:286
  49.0 6.6 %collective-permute-start.4 = (f32[128,256]{1,0:T(8,128)S(1)}, f32[128,256]{1,0:T(8,128)S(1)}, u32[]{:S(2)}, u32[]{:S(2)}) collective-permute-start(f32[128,256]{1,0:T(8,128)S(1)} %fusion.4), channel_id=1, source_target_pairs={{0,12},{4,0},{8,4},{12,8},{1,13},{5,1},{9,5},{13,9},{2,14},{6,2},{... | collective-permute-start | bytes 393224 | tf_op jit(solution)/shard_map/ppermute | solution.py:286
  51.8 6.6 %collective-permute-start.5 = (f32[128,256]{1,0:T(8,128)S(1)}, f32[128,256]{1,0:T(8,128)S(1)}, u32[]{:S(2)}, u32[]{:S(2)}) collective-permute-start(f32[128,256]{1,0:T(8,128)S(1)} %fusion.4), channel_id=1, source_target_pairs={{0,8},{4,12},{8,0},{12,4},{1,9},{5,13},{9,1},{13,5},{2,10},{6,14},... | collective-permute-start | bytes 393224 | tf_op jit(solution)/shard_map/ppermute | solution.py:286
  52.7 6.9 %collective-permute-start.6 = (f32[128,256]{1,0:T(8,128)S(1)}, f32[128,256]{1,0:T(8,128)S(1)}, u32[]{:S(2)}, u32[]{:S(2)}) collective-permute-start(f32[128,256]{1,0:T(8,128)S(1)} %fusion.4), channel_id=1, source_target_pairs={{0,4},{4,8},{8,12},{12,0},{1,5},{5,9},{9,13},{13,1},{2,6},{6,10},{... | collective-permute-start | bytes 393224 | tf_op jit(solution)/shard_map/ppermute | solution.py:286
  59.8 2.0 %collective-permute-start.7 = (f32[512,256]{1,0:T(8,128)S(1)}, f32[512,256]{1,0:T(8,128)S(1)}, u32[]{:S(2)}, u32[]{:S(2)}) collective-permute-start(f32[512,256]{1,0:T(8,128)S(1)} %bitcast.70), channel_id=1, source_target_pairs={{0,1},{1,0},{2,3},{3,2},{4,5},{5,4},{6,7},{7,6},{8,9},{9,8},{10,11... | collective-permute-start | bytes 1572872 | tf_op jit(solution)/shard_map/ppermute | solution.py:286
  59.9 35.1 %copy-start = (bf16[288,256]{1,0:T(8,128)(2,1)S(1)}, bf16[288,256]{1,0:T(8,128)(2,1)}, u32[]{:S(2)}) copy-start(bf16[288,256]{1,0:T(8,128)(2,1)} %plane_ref.1) | copy-start | bytes 442372
  133.8 2.3 %collective-permute-start.12 = (bf16[1024,256]{1,0:T(8,128)(2,1)S(1)}, bf16[1024,256]{1,0:T(8,128)(2,1)S(1)}, u32[]{:S(2)}, u32[]{:S(2)}) collective-permute-start(bf16[1024,256]{1,0:T(8,128)(2,1)S(1)} %slice.4), channel_id=1, source_target_pairs={{0,1},{1,0},{2,3},{3,2},{4,5},{5,4},{6,7},{7,6},{8,9},{9,8},{10,11... | collective-permute-start | bytes 1572872 | tf_op jit(solution)/shard_map/ppermute | solution.py:286

commit v4 on v3

--- a/solution.py
+++ b/solution.py
@@ -90,13 +90,14 @@
 
 def first_basis_kernel(s_ref, basis_ref, a_ref, m_ref):
     places = [
-        ((c * 4 + z) * 2 + yh) * 2 + yl
+        (((c * 4 + x) * 4 + z) * 2 + yh) * 2 + yl
         for z in range(4)
         for yh in range(2)
+        for x in range(4)
         for yl in range(2)
         for c in range(2)
     ]
-    s = jnp.concatenate([s_ref[place * 32 : place * 32 + 32] for place in places], axis=0)
+    s = jnp.concatenate([s_ref[place * 8 : place * 8 + 8] for place in places], axis=0)
     inverse_factor(s, basis_ref, a_ref, m_ref, False)
 
 
@@ -314,7 +315,7 @@
     rows = first_sums(tensor, omega_two, omega_three)
     some_rank = collect(sketch_rank, "yl")
 
-    parts = exchange(rows.reshape(4, -1, rank), ("yl", "c"))
+    parts = exchange(rows.reshape(n_sa, -1, rank), SA)
     rows, some_rank = lax.optimization_barrier((jnp.sum(parts, axis=0), some_rank))
     rows = gather(rows, AF + ("yl",), n_af * 2)
 
@@ -322,12 +323,6 @@
     pieces = jnp.swapaxes(tensor, 1, 2).reshape(n_af, fine_rows, planes, local_cols)
     moved = exchange(pieces, AF)
 
-    n_x, at = lax.axis_size("x"), lax.axis_index("x")
-    shares = rows.reshape(n_x, -1, rank)
-    rows = lax.dynamic_index_in_dim(shares, at, 0, keepdims=False)
-    for step in range(1, n_x):
-        share = lax.dynamic_index_in_dim(shares, (at + step) % n_x, 0, keepdims=False)
-        rows = rows + around(share, "x", step)
     rows = collect(collect(rows, "x"), "c")
     whole_rank = collect(collect(some_rank, "c"), "x").reshape(4, 2, 2, -1, rank)
     whole_rank = whole_rank.swapaxes(1, 2).reshape(rank, rank)

time: 158 us -> 155 us (0.981)
  starting transfers between devices: 32.3 us -> 18.2 us
  blocking collectives: 45.5 us -> 59.3 us
  waiting for transfers between devices: 50.8 us -> 48.8 us
    all_to_all x2 -> x3, blocking collectives: 45.5 us -> 59.3 us  [exchange(): return lax.all_to_all(blocks, axes, split_axis=0, concat_axis=0, tiled=True)]
    ppermute x13 -> x10, starting transfers between devices: 16.6 us -> 8.12 us  [around(): lax.ppermute(block, axes, [(p, (p + step) % count) for p in range(count)])]
    all_to_all x3 -> x2, starting transfers between devices: 15.7 us -> 10.1 us  [exchange(): return lax.all_to_all(blocks, axes, split_axis=0, concat_axis=0, tiled=True)]
    all_to_all x3 -> x2, waiting for transfers between devices: 36 us -> 30.5 us  [exchange(): return lax.all_to_all(blocks, axes, split_axis=0, concat_axis=0, tiled=True)]
    ppermute x13 -> x10, waiting for transfers between devices: 14.8 us -> 18.4 us  [around(): lax.ppermute(block, axes, [(p, (p + step) % count) for p in range(count)])]
  transfers between devices with their start and end apart: 16 -> 12, of which waited for: 12 -> 12; matrix products, arithmetic and copies ran while one was open for 0% -> 0% of each run, Pallas kernels for 8% -> 4%
where the time goes in v4:
time: 155 us; the launch traced here: 154 us
  blocking collectives  59.3 us (38%)
  waiting for transfers between devices  48.8 us (31%)
  Pallas kernels  27.3 us (18%)
  starting transfers between devices  18.2 us (12%)
    all_to_all x3, blocking collectives, exchange(): return lax.all_to_all(blocks, axes, split_axis=0, concat_axis=0, tiled=True)  59.3 us
    all_to_all x2, waiting for transfers between devices, exchange(): return lax.all_to_all(blocks, axes, split_axis=0, concat_axis=0, tiled=True)  30.5 us
    ppermute x10, waiting for transfers between devices, around(): lax.ppermute(block, axes, [(p, (p + step) % count) for p in range(count)])  18.4 us
    all_to_all x2, starting transfers between devices, exchange(): return lax.all_to_all(blocks, axes, split_axis=0, concat_axis=0, tiled=True)  10.1 us
    ppermute x10, starting transfers between devices, around(): lax.ppermute(block, axes, [(p, (p + step) % count) for p in range(count)])  8.12 us
    pallas_call x1, Pallas kernels, second_core(): pl.pallas_call(second_core_kernel, out_shape=jax.ShapeDtypeStruct((n, lan...  6.98 us
    pallas_call x1, Pallas kernels, first_basis(): pl.pallas_call(first_basis_kernel, out_shape=jax.ShapeDtypeStruct(sketch....  6.9 us
    pallas_call x1, Pallas kernels, project(): pl.pallas_call(project_kernel, out_shape=jax.ShapeDtypeStruct((rank // 2...  6.54 us
  transfers between devices with their start and end apart: 12, of which 12 were waited for; matrix products, arithmetic and copies ran while one was open for 0% of the time, Pallas kernels for 4%

profile of v4, /device:TPU:0, one launch (start us, length us, event | category | flops | bytes accessed | tf_op | source)
XLA Modules:
  0.0 154.3 jit_solution(16738032150759273800)
XLA Ops:
  0.0 5.6 %first_sums.1 = f32[128,256]{1,0:T(8,128)} custom-call(bf16[64,256]{1,0:T(8,128)(2,1)} %two_ref.1, bf16[288,256]{1,0:T(8,128)(2,1)} %three_ref.1, bf16[64,288,128]{2,1,0:T(8,128)(2,1)} %bitcast.55), custom_call_target="tpu_custom_call" | custom-call | flops 1000000000 | bytes 5000000 | tf_op jit(solution)/shard_map/first_sums/pallas_call | solution.py:165
  5.6 5.5 %all-to-all-start = ((f32[16,8,256]{2,1,0:T(8,128)}), f32[16,8,256]{2,1,0:T(8,128)S(1)}, u32[]{:S(2)}, u32[]{:S(2)}) async-start(f32[16,8,256]{2,1,0:T(8,128)} %bitcast.65), calls=%async_computation | async-start | bytes 262144 | tf_op jit(solution)/shard_map/all_to_all | solution.py:277
  11.2 2.0 %collective-permute-start = (bf16[16,256]{1,0:T(8,128)(2,1)S(1)}, bf16[16,256]{1,0:T(8,128)(2,1)S(1)}, u32[]{:S(2)}, u32[]{:S(2)}) collective-permute-start(bf16[16,256]{1,0:T(8,128)(2,1)S(1)} %copy-done.1), channel_id=1, source_target_pairs={{0,2},{2,0},{1,3},{3,1},{4,6},{6,4},{5,7},{7,5},{8,10},{10,8},{9,1... | collective-permute-start | bytes 24584 | tf_op jit(solution)/shard_map/ppermute | solution.py:287
  13.2 1.9 %collective-permute-done = bf16[16,256]{1,0:T(8,128)(2,1)S(1)} collective-permute-done((bf16[16,256]{1,0:T(8,128)(2,1)S(1)}, bf16[16,256]{1,0:T(8,128)(2,1)S(1)}, u32[]{:S(2)}, u32[]{:S(2)}) %collective-permute-start) | collective-permute-done | bytes 8224 | tf_op jit(solution)/shard_map/ppermute | solution.py:287
  15.1 2.5 %all-to-all-done = f32[16,8,256]{2,1,0:T(8,128)S(1)} async-done(((f32[16,8,256]{2,1,0:T(8,128)}), f32[16,8,256]{2,1,0:T(8,128)S(1)}, u32[]{:S(2)}, u32[]{:S(2)}) %all-to-all-start) | async-done | bytes 131104 | tf_op jit(solution)/shard_map/all_to_all | solution.py:277
  17.7 15.5 %all_to_all.25 = f32[16,8,256]{2,1,0:T(8,128)S(1)} all-to-all(f32[16,8,256]{2,1,0:T(8,128)S(1)} %broadcast_in_dim.2), channel_id=1, replica_groups=mesh['z'=4,'yh'=2,'x'=4,'yl'=2,'c'=2] {'z','yh','yl'}, dimensions={0} | all-to-all | bytes 262144 | tf_op jit(solution)/shard_map/all_to_all | solution.py:277
  33.2 4.6 %all-to-all-start.2 = ((bf16[8,8,288,128]{3,2,1,0:T(8,128)(2,1)}), bf16[8,8,288,128]{3,2,1,0:T(8,128)(2,1)}, u32[]{:S(2)}, u32[]{:S(2)}) async-start(bf16[8,8,288,128]{3,2,1,0:T(8,128)(2,1)} %bitcast.56), calls=%async_computation.2 | async-start | bytes 9437184 | tf_op jit(solution)/shard_map/all_to_all | solution.py:277
  37.8 0.1 collective-permute-start.5
  37.9 1.2 collective-permute-done.5
  39.1 1.1 collective-permute-start.6
  40.2 1.3 collective-permute-start.7
  41.5 0.3 collective-permute-start.8
  41.8 1.3 collective-permute-done.6
  43.1 2.7 %collective-permute-done.7 = bf16[64,256]{1,0:T(8,128)(2,1)S(1)} collective-permute-done((bf16[64,256]{1,0:T(8,128)(2,1)S(1)}, bf16[64,256]{1,0:T(8,128)(2,1)S(1)}, u32[]{:S(2)}, u32[]{:S(2)}) %collective-permute-start.7) | collective-permute-done | bytes 32800 | tf_op jit(solution)/shard_map/ppermute | solution.py:287
  45.8 0.9 collective-permute-done.8
  46.7 1.2 collective-permute-start.1
  47.9 0.9 collective-permute-start.2
  48.8 0.4 collective-permute-start.3
  49.2 3.2 %collective-permute-done.1 = f32[128,256]{1,0:T(8,128)S(1)} collective-permute-done((f32[128,256]{1,0:T(8,128)S(1)}, f32[128,256]{1,0:T(8,128)S(1)}, u32[]{:S(2)}, u32[]{:S(2)}) %collective-permute-start.1) | collective-permute-done | bytes 131104 | tf_op jit(solution)/shard_map/ppermute | solution.py:287
  52.4 2.5 %collective-permute-done.2 = f32[128,256]{1,0:T(8,128)S(1)} collective-permute-done((f32[128,256]{1,0:T(8,128)S(1)}, f32[128,256]{1,0:T(8,128)S(1)}, u32[]{:S(2)}, u32[]{:S(2)}) %collective-permute-start.2) | collective-permute-done | bytes 131104 | tf_op jit(solution)/shard_map/ppermute | solution.py:287
  55.0 1.3 collective-permute-done.3
  56.6 1.8 %collective-permute-done.4 = f32[512,256]{1,0:T(8,128)S(1)} collective-permute-done((f32[512,256]{1,0:T(8,128)S(1)}, f32[512,256]{1,0:T(8,128)S(1)}, u32[]{:S(2)}, u32[]{:S(2)}) %collective-permute-start.4) | collective-permute-done | bytes 524320 | tf_op jit(solution)/shard_map/ppermute | solution.py:287
  58.4 0.2 fusion.2
  58.6 6.9 %first_basis.1.basis_ref = bf16[1024,256]{1,0:T(8,128)(2,1)S(1)} custom-call(f32[1024,256]{1,0:T(8,128)S(1)} %bitcast.49), custom_call_target="tpu_custom_call" | custom-call | tf_op jit(solution)/shard_map/first_basis/pallas_call | solution.py:106
  65.6 28.0 %all-to-all-done.2.moved_ref = bf16[8,8,288,128]{3,2,1,0:T(8,128)(2,1)} async-done(((bf16[8,8,288,128]{3,2,1,0:T(8,128)(2,1)}), bf16[8,8,288,128]{3,2,1,0:T(8,128)(2,1)}, u32[]{:S(2)}, u32[]{:S(2)}) %all-to-all-start.2) | async-done | bytes 4718624 | tf_op jit(solution)/shard_map/all_to_all | solution.py:277
  93.5 6.5 %project.1 = bf16[1024,896]{1,0:T(8,128)(2,1)S(1)} custom-call(bf16[1024,256]{1,0:T(8,128)(2,1)S(1)} %first_basis.1.basis_ref, bf16[288,256]{1,0:T(8,128)(2,1)S(1)} %copy-done, bf16[256,256]{1,0:T(8,128)(2,1)S(1)} %bitcast.54, bf16[8,8,288,128]{3,2,1,0:T(8,128)(2,1)} %all-to-all-done.2.moved_ref), custom_call_target="tpu_custom_call" | custom-call | flops 2000000000 | bytes 8000000 | tf_op jit(solution)/shard_map/project/pallas_call | solution.py:225
  100.1 30.5 %all_to_all.26 = bf16[128,8,896]{2,1,0:T(8,128)(2,1)S(1)} all-to-all(bf16[128,8,896]{2,1,0:T(8,128)(2,1)S(1)} %bitcast.52), channel_id=1, replica_groups=mesh['z'=4,'yh'=2,'x'=4,'yl'=2,'c'=2] {'x','yl','c','z','yh'}, dimensions={0} | all-to-all | bytes 3670016 | tf_op jit(solution)/shard_map/all_to_all | solution.py:277
  130.6 0.8 collective-permute-start.9
  131.4 1.5 collective-permute-done.9.other_ref
  132.9 7.0 %second_core.1 = bf16[256,640]{1,0:T(8,128)(2,1)S(1)} custom-call(bf16[1024,896]{1,0:T(8,128)(2,1)S(1)} %bitcast.51, bf16[1024,256]{1,0:T(8,128)(2,1)S(1)} %collective-permute-done.9.other_ref), custom_call_target="tpu_custom_call" | custom-call | flops 4000000000 | bytes 3000000 | tf_op jit(solution)/shard_map/second_core/pallas_call | solution.py:128
  139.9 13.2 %all_to_all.27.got_ref = bf16[8,32,640]{2,1,0:T(8,128)(2,1)S(1)} all-to-all(bf16[8,32,640]{2,1,0:T(8,128)(2,1)S(1)} %bitcast.53), channel_id=1, replica_groups=mesh['z'=4,'yh'=2,'x'=4,'yl'=2,'c'=2] {'z','yh'}, dimensions={0} | all-to-all | bytes 655360 | tf_op jit(solution)/shard_map/all_to_all | solution.py:277
  153.1 1.2 merge.1
  (29 shorter events, 0.4 us)
Async XLA Ops:
  0.0 11.2 %copy-start.1 = (bf16[16,256]{1,0:T(8,128)(2,1)S(1)}, bf16[16,256]{1,0:T(8,128)(2,1)}, u32[]{:S(2)}) copy-start(bf16[16,256]{1,0:T(8,128)(2,1)} %param.8) | copy-start | bytes 24580
  5.6 12.0 %all-to-all-start = ((f32[16,8,256]{2,1,0:T(8,128)}), f32[16,8,256]{2,1,0:T(8,128)S(1)}, u32[]{:S(2)}, u32[]{:S(2)}) async-start(f32[16,8,256]{2,1,0:T(8,128)} %bitcast.65), calls=%async_computation | async-start | bytes 262144 | tf_op jit(solution)/shard_map/all_to_all | solution.py:277
  11.2 3.9 %collective-permute-start = (bf16[16,256]{1,0:T(8,128)(2,1)S(1)}, bf16[16,256]{1,0:T(8,128)(2,1)S(1)}, u32[]{:S(2)}, u32[]{:S(2)}) collective-permute-start(bf16[16,256]{1,0:T(8,128)(2,1)S(1)} %copy-done.1), channel_id=1, source_target_pairs={{0,2},{2,0},{1,3},{3,1},{4,6},{6,4},{5,7},{7,5},{8,10},{10,8},{9,1... | collective-permute-start | bytes 24584 | tf_op jit(solution)/shard_map/ppermute | solution.py:287
  33.2 60.3 %all-to-all-start.2 = ((bf16[8,8,288,128]{3,2,1,0:T(8,128)(2,1)}), bf16[8,8,288,128]{3,2,1,0:T(8,128)(2,1)}, u32[]{:S(2)}, u32[]{:S(2)}) async-start(bf16[8,8,288,128]{3,2,1,0:T(8,128)(2,1)} %bitcast.56), calls=%async_computation.2 | async-start | bytes 9437184 | tf_op jit(solution)/shard_map/all_to_all | solution.py:277
  37.8 1.3 collective-permute-start.5
  39.1 4.0 %collective-permute-start.6 = (bf16[64,256]{1,0:T(8,128)(2,1)S(1)}, bf16[64,256]{1,0:T(8,128)(2,1)S(1)}, u32[]{:S(2)}, u32[]{:S(2)}) collective-permute-start(bf16[64,256]{1,0:T(8,128)(2,1)S(1)} %bitcast.67), channel_id=1, source_target_pairs={{0,12},{4,0},{8,4},{12,8},{1,13},{5,1},{9,5},{13,9},{2,14},{6,2},{... | collective-permute-start | bytes 98312 | tf_op jit(solution)/shard_map/ppermute | solution.py:287
  40.2 5.5 %collective-permute-start.7 = (bf16[64,256]{1,0:T(8,128)(2,1)S(1)}, bf16[64,256]{1,0:T(8,128)(2,1)S(1)}, u32[]{:S(2)}, u32[]{:S(2)}) collective-permute-start(bf16[64,256]{1,0:T(8,128)(2,1)S(1)} %bitcast.68), channel_id=1, source_target_pairs={{0,8},{4,12},{8,0},{12,4},{1,9},{5,13},{9,1},{13,5},{2,10},{6,14},... | collective-permute-start | bytes 98312 | tf_op jit(solution)/shard_map/ppermute | solution.py:287
  41.5 5.1 %collective-permute-start.8 = (bf16[64,256]{1,0:T(8,128)(2,1)S(1)}, bf16[64,256]{1,0:T(8,128)(2,1)S(1)}, u32[]{:S(2)}, u32[]{:S(2)}) collective-permute-start(bf16[64,256]{1,0:T(8,128)(2,1)S(1)} %bitcast.69), channel_id=1, source_target_pairs={{0,4},{4,8},{8,12},{12,0},{1,5},{5,9},{9,13},{13,1},{2,6},{6,10},{... | collective-permute-start | bytes 98312 | tf_op jit(solution)/shard_map/ppermute | solution.py:287
  46.7 5.7 %collective-permute-start.1 = (f32[128,256]{1,0:T(8,128)S(1)}, f32[128,256]{1,0:T(8,128)S(1)}, u32[]{:S(2)}, u32[]{:S(2)}) collective-permute-start(f32[128,256]{1,0:T(8,128)S(1)} %bitcast.59), channel_id=1, source_target_pairs={{0,12},{4,0},{8,4},{12,8},{1,13},{5,1},{9,5},{13,9},{2,14},{6,2},{... | collective-permute-start | bytes 393224 | tf_op jit(solution)/shard_map/ppermute | solution.py:287
  47.9 7.1 %collective-permute-start.2 = (f32[128,256]{1,0:T(8,128)S(1)}, f32[128,256]{1,0:T(8,128)S(1)}, u32[]{:S(2)}, u32[]{:S(2)}) collective-permute-start(f32[128,256]{1,0:T(8,128)S(1)} %bitcast.60), channel_id=1, source_target_pairs={{0,8},{4,12},{8,0},{12,4},{1,9},{5,13},{9,1},{13,5},{2,10},{6,14},... | collective-permute-start | bytes 393224 | tf_op jit(solution)/shard_map/ppermute | solution.py:287
  48.8 7.5 %collective-permute-start.3 = (f32[128,256]{1,0:T(8,128)S(1)}, f32[128,256]{1,0:T(8,128)S(1)}, u32[]{:S(2)}, u32[]{:S(2)}) collective-permute-start(f32[128,256]{1,0:T(8,128)S(1)} %bitcast.61), channel_id=1, source_target_pairs={{0,4},{4,8},{8,12},{12,0},{1,5},{5,9},{9,13},{13,1},{2,6},{6,10},{... | collective-permute-start | bytes 393224 | tf_op jit(solution)/shard_map/ppermute | solution.py:287
  56.4 2.0 %collective-permute-start.4 = (f32[512,256]{1,0:T(8,128)S(1)}, f32[512,256]{1,0:T(8,128)S(1)}, u32[]{:S(2)}, u32[]{:S(2)}) collective-permute-start(f32[512,256]{1,0:T(8,128)S(1)} %bitcast.57), channel_id=1, source_target_pairs={{0,1},{1,0},{2,3},{3,2},{4,5},{5,4},{6,7},{7,6},{8,9},{9,8},{10,11... | collective-permute-start | bytes 1572872 | tf_op jit(solution)/shard_map/ppermute | solution.py:287
  56.6 37.0 %copy-start = (bf16[288,256]{1,0:T(8,128)(2,1)S(1)}, bf16[288,256]{1,0:T(8,128)(2,1)}, u32[]{:S(2)}) copy-start(bf16[288,256]{1,0:T(8,128)(2,1)} %plane_ref.1) | copy-start | bytes 442372
  130.6 2.3 %collective-permute-start.9 = (bf16[1024,256]{1,0:T(8,128)(2,1)S(1)}, bf16[1024,256]{1,0:T(8,128)(2,1)S(1)}, u32[]{:S(2)}, u32[]{:S(2)}) collective-permute-start(bf16[1024,256]{1,0:T(8,128)(2,1)S(1)} %slice.4), channel_id=1, source_target_pairs={{0,1},{1,0},{2,3},{3,2},{4,5},{5,4},{6,7},{7,6},{8,9},{9,8},{10,11... | collective-permute-start | bytes 1572872 | tf_op jit(solution)/shard_map/ppermute | solution.py:287

commit v5 on v4

--- a/solution.py
+++ b/solution.py
@@ -22,6 +22,15 @@
     return x.astype(jnp.bfloat16)
 
 
+def halves_of(x):
+    upper = low(x)
+    return upper, low(x - upper.astype(jnp.float32))
+
+
+def fine(a, b, dims=NN):
+    return mm(a[0], b[0], dims) + (mm(a[0], b[1], dims) + mm(a[1], b[0], dims))
+
+
 def inverse_factor(s, basis_ref, a_ref, m_ref, turned):
     n = s.shape[1]
     row = lax.broadcasted_iota(jnp.int32, (n, n), 0)
@@ -30,9 +39,11 @@
     one = jnp.where(eye, 1.0, 0.0)
     half = jnp.where(row > col, 1.0, 0.5 * one)
 
+    sketch = halves_of(s)
+
     def put(inverse):
-        basis = mm(inverse, s, NT, HIGH) if turned else mm(s, inverse, NT, HIGH)
-        basis_ref[...] = low(basis)
+        inverse = halves_of(inverse)
+        basis_ref[...] = low(fine(inverse, sketch, NT) if turned else fine(sketch, inverse, NT))
 
     gram = mm(s, s, TN, HIGH)
     on_diag = jnp.where(eye, gram, 0.0)
@@ -51,9 +62,11 @@
         if step < early - 1:
             h = mm(low(mm(kb, low(h))), kb, NT)
     m = m.astype(jnp.float32)
+    gram = halves_of(scaled)
     for _ in range(2):
-        r = mm(mm(m, scaled, NN, HIGH), m, NT, HIGH) - one
-        m = m - mm(half * r, m, NN, HIGH)
+        both = halves_of(m)
+        r = fine(halves_of(fine(both, gram)), both, NT) - one
+        m = m - fine(halves_of(half * r), both)
     good = jnp.logical_and(jnp.sum(r * r) < 1e-3, jnp.min(jnp.where(eye, m, 1.0)) > 0.0)
     put(m * inv_row)
 

time: 155 us -> 153 us (0.987)
  Pallas kernels: 27.3 us -> 24.1 us
  waiting for transfers between devices: 48.8 us -> 50.6 us
    pallas_call x1, Pallas kernels: 6.9 us -> 5.17 us  [first_basis(): pl.pallas_call(first_basis_kernel, out_shape=jax.ShapeDtypeStruct(sketch....]
    all_to_all x2, waiting for transfers between devices: 30.5 us -> 32.2 us  [exchange(): return lax.all_to_all(blocks, axes, split_axis=0, concat_axis=0, tiled=True)]
  transfers between devices with their start and end apart: 12 -> 12, of which waited for: 12 -> 12; matrix products, arithmetic and copies ran while one was open for 0% -> 0% of each run, Pallas kernels for 4% -> 3%
where the time goes in v5:
time: 153 us
  blocking collectives  59.2 us (39%)
  waiting for transfers between devices  50.6 us (33%)
  Pallas kernels  24.1 us (16%)
  starting transfers between devices  18.2 us (12%)
    all_to_all x3, blocking collectives, exchange(): return lax.all_to_all(blocks, axes, split_axis=0, concat_axis=0, tiled=True)  59.2 us
    all_to_all x2, waiting for transfers between devices, exchange(): return lax.all_to_all(blocks, axes, split_axis=0, concat_axis=0, tiled=True)  32.2 us
    ppermute x10, waiting for transfers between devices, around(): lax.ppermute(block, axes, [(p, (p + step) % count) for p in range(count)])  18.4 us
    all_to_all x2, starting transfers between devices, exchange(): return lax.all_to_all(blocks, axes, split_axis=0, concat_axis=0, tiled=True)  10.1 us
    ppermute x10, starting transfers between devices, around(): lax.ppermute(block, axes, [(p, (p + step) % count) for p in range(count)])  8.12 us
    pallas_call x1, Pallas kernels, project(): pl.pallas_call(project_kernel, out_shape=jax.ShapeDtypeStruct((rank // 2...  6.54 us
    pallas_call x1, Pallas kernels, first_sums(): pl.pallas_call(first_sums_kernel, grid=(rows // count,), out_shape=jax.Sh...  5.64 us
    pallas_call x1, Pallas kernels, second_core(): pl.pallas_call(second_core_kernel, out_shape=jax.ShapeDtypeStruct((n, lan...  5.52 us
  transfers between devices with their start and end apart: 12, of which 12 were waited for; matrix products, arithmetic and copies ran while one was open for 0% of the time, Pallas kernels for 3%

profile of v5, /device:TPU:0, one launch (start us, length us, event | category | flops | bytes accessed | tf_op | source)
XLA Modules:
  0.0 152.9 jit_solution(12766402486964737814)
XLA Ops:
  0.0 5.6 %first_sums.1 = f32[128,256]{1,0:T(8,128)} custom-call(bf16[64,256]{1,0:T(8,128)(2,1)} %two_ref.1, bf16[288,256]{1,0:T(8,128)(2,1)} %three_ref.1, bf16[64,288,128]{2,1,0:T(8,128)(2,1)} %bitcast.55), custom_call_target="tpu_custom_call" | custom-call | flops 1000000000 | bytes 5000000 | tf_op jit(solution)/shard_map/first_sums/pallas_call | solution.py:178
  5.6 5.5 %all-to-all-start = ((f32[16,8,256]{2,1,0:T(8,128)}), f32[16,8,256]{2,1,0:T(8,128)S(1)}, u32[]{:S(2)}, u32[]{:S(2)}) async-start(f32[16,8,256]{2,1,0:T(8,128)} %bitcast.65), calls=%async_computation | async-start | bytes 262144 | tf_op jit(solution)/shard_map/all_to_all | solution.py:290
  11.2 2.0 %collective-permute-start = (bf16[16,256]{1,0:T(8,128)(2,1)S(1)}, bf16[16,256]{1,0:T(8,128)(2,1)S(1)}, u32[]{:S(2)}, u32[]{:S(2)}) collective-permute-start(bf16[16,256]{1,0:T(8,128)(2,1)S(1)} %copy-done.1), channel_id=1, source_target_pairs={{0,2},{2,0},{1,3},{3,1},{4,6},{6,4},{5,7},{7,5},{8,10},{10,8},{9,1... | collective-permute-start | bytes 24584 | tf_op jit(solution)/shard_map/ppermute | solution.py:300
  13.2 1.9 %collective-permute-done = bf16[16,256]{1,0:T(8,128)(2,1)S(1)} collective-permute-done((bf16[16,256]{1,0:T(8,128)(2,1)S(1)}, bf16[16,256]{1,0:T(8,128)(2,1)S(1)}, u32[]{:S(2)}, u32[]{:S(2)}) %collective-permute-start) | collective-permute-done | bytes 8224 | tf_op jit(solution)/shard_map/ppermute | solution.py:300
  15.1 2.5 %all-to-all-done = f32[16,8,256]{2,1,0:T(8,128)S(1)} async-done(((f32[16,8,256]{2,1,0:T(8,128)}), f32[16,8,256]{2,1,0:T(8,128)S(1)}, u32[]{:S(2)}, u32[]{:S(2)}) %all-to-all-start) | async-done | bytes 131104 | tf_op jit(solution)/shard_map/all_to_all | solution.py:290
  17.7 15.5 %all_to_all.25 = f32[16,8,256]{2,1,0:T(8,128)S(1)} all-to-all(f32[16,8,256]{2,1,0:T(8,128)S(1)} %broadcast_in_dim.2), channel_id=1, replica_groups=mesh['z'=4,'yh'=2,'x'=4,'yl'=2,'c'=2] {'z','yh','yl'}, dimensions={0} | all-to-all | bytes 262144 | tf_op jit(solution)/shard_map/all_to_all | solution.py:290
  33.2 4.6 %all-to-all-start.2 = ((bf16[8,8,288,128]{3,2,1,0:T(8,128)(2,1)}), bf16[8,8,288,128]{3,2,1,0:T(8,128)(2,1)}, u32[]{:S(2)}, u32[]{:S(2)}) async-start(bf16[8,8,288,128]{3,2,1,0:T(8,128)(2,1)} %bitcast.56), calls=%async_computation.2 | async-start | bytes 9437184 | tf_op jit(solution)/shard_map/all_to_all | solution.py:290
  37.8 0.1 collective-permute-start.5
  37.9 1.2 collective-permute-done.5
  39.1 1.1 collective-permute-start.6
  40.2 1.3 collective-permute-start.7
  41.5 0.3 collective-permute-start.8
  41.8 1.3 collective-permute-done.6
  43.1 2.7 %collective-permute-done.7 = bf16[64,256]{1,0:T(8,128)(2,1)S(1)} collective-permute-done((bf16[64,256]{1,0:T(8,128)(2,1)S(1)}, bf16[64,256]{1,0:T(8,128)(2,1)S(1)}, u32[]{:S(2)}, u32[]{:S(2)}) %collective-permute-start.7) | collective-permute-done | bytes 32800 | tf_op jit(solution)/shard_map/ppermute | solution.py:300
  45.8 0.9 collective-permute-done.8
  46.7 1.2 collective-permute-start.1
  47.9 0.9 collective-permute-start.2
  48.8 0.4 collective-permute-start.3
  49.2 3.2 %collective-permute-done.1 = f32[128,256]{1,0:T(8,128)S(1)} collective-permute-done((f32[128,256]{1,0:T(8,128)S(1)}, f32[128,256]{1,0:T(8,128)S(1)}, u32[]{:S(2)}, u32[]{:S(2)}) %collective-permute-start.1) | collective-permute-done | bytes 131104 | tf_op jit(solution)/shard_map/ppermute | solution.py:300
  52.4 2.5 %collective-permute-done.2 = f32[128,256]{1,0:T(8,128)S(1)} collective-permute-done((f32[128,256]{1,0:T(8,128)S(1)}, f32[128,256]{1,0:T(8,128)S(1)}, u32[]{:S(2)}, u32[]{:S(2)}) %collective-permute-start.2) | collective-permute-done | bytes 131104 | tf_op jit(solution)/shard_map/ppermute | solution.py:300
  55.0 1.3 collective-permute-done.3
  56.6 1.8 %collective-permute-done.4 = f32[512,256]{1,0:T(8,128)S(1)} collective-permute-done((f32[512,256]{1,0:T(8,128)S(1)}, f32[512,256]{1,0:T(8,128)S(1)}, u32[]{:S(2)}, u32[]{:S(2)}) %collective-permute-start.4) | collective-permute-done | bytes 524320 | tf_op jit(solution)/shard_map/ppermute | solution.py:300
  58.4 0.2 fusion.2
  58.6 5.2 %first_basis.1.basis_ref = bf16[1024,256]{1,0:T(8,128)(2,1)S(1)} custom-call(f32[1024,256]{1,0:T(8,128)S(1)} %bitcast.49), custom_call_target="tpu_custom_call" | custom-call | tf_op jit(solution)/shard_map/first_basis/pallas_call | solution.py:119
  63.8 29.7 %all-to-all-done.2.moved_ref = bf16[8,8,288,128]{3,2,1,0:T(8,128)(2,1)} async-done(((bf16[8,8,288,128]{3,2,1,0:T(8,128)(2,1)}), bf16[8,8,288,128]{3,2,1,0:T(8,128)(2,1)}, u32[]{:S(2)}, u32[]{:S(2)}) %all-to-all-start.2) | async-done | bytes 4718624 | tf_op jit(solution)/shard_map/all_to_all | solution.py:290
  93.5 6.5 %project.1 = bf16[1024,896]{1,0:T(8,128)(2,1)S(1)} custom-call(bf16[1024,256]{1,0:T(8,128)(2,1)S(1)} %first_basis.1.basis_ref, bf16[288,256]{1,0:T(8,128)(2,1)S(1)} %copy-done, bf16[256,256]{1,0:T(8,128)(2,1)S(1)} %bitcast.54, bf16[8,8,288,128]{3,2,1,0:T(8,128)(2,1)} %all-to-all-done.2.moved_ref), custom_call_target="tpu_custom_call" | custom-call | flops 2000000000 | bytes 8000000 | tf_op jit(solution)/shard_map/project/pallas_call | solution.py:238
  100.1 30.5 %all_to_all.26 = bf16[128,8,896]{2,1,0:T(8,128)(2,1)S(1)} all-to-all(bf16[128,8,896]{2,1,0:T(8,128)(2,1)S(1)} %bitcast.52), channel_id=1, replica_groups=mesh['z'=4,'yh'=2,'x'=4,'yl'=2,'c'=2] {'x','yl','c','z','yh'}, dimensions={0} | all-to-all | bytes 3670016 | tf_op jit(solution)/shard_map/all_to_all | solution.py:290
  130.6 0.8 collective-permute-start.9
  131.4 1.5 %collective-permute-done.9.other_ref = bf16[1024,256]{1,0:T(8,128)(2,1)S(1)} collective-permute-done((bf16[1024,256]{1,0:T(8,128)(2,1)S(1)}, bf16[1024,256]{1,0:T(8,128)(2,1)S(1)}, u32[]{:S(2)}, u32[]{:S(2)}) %collective-permute-start.9) | collective-permute-done | bytes 524320 | tf_op jit(solution)/shard_map/ppermute | solution.py:300
  132.9 5.5 %second_core.1 = bf16[256,640]{1,0:T(8,128)(2,1)S(1)} custom-call(bf16[1024,896]{1,0:T(8,128)(2,1)S(1)} %bitcast.51, bf16[1024,256]{1,0:T(8,128)(2,1)S(1)} %collective-permute-done.9.other_ref), custom_call_target="tpu_custom_call" | custom-call | flops 4000000000 | bytes 3000000 | tf_op jit(solution)/shard_map/second_core/pallas_call | solution.py:141
  138.5 13.2 %all_to_all.27.got_ref = bf16[8,32,640]{2,1,0:T(8,128)(2,1)S(1)} all-to-all(bf16[8,32,640]{2,1,0:T(8,128)(2,1)S(1)} %bitcast.53), channel_id=1, replica_groups=mesh['z'=4,'yh'=2,'x'=4,'yl'=2,'c'=2] {'z','yh'}, dimensions={0} | all-to-all | bytes 655360 | tf_op jit(solution)/shard_map/all_to_all | solution.py:290
  151.7 1.2 merge.1
  (29 shorter events, 0.4 us)
Async XLA Ops:
  0.0 11.2 %copy-start.1 = (bf16[16,256]{1,0:T(8,128)(2,1)S(1)}, bf16[16,256]{1,0:T(8,128)(2,1)}, u32[]{:S(2)}) copy-start(bf16[16,256]{1,0:T(8,128)(2,1)} %param.8) | copy-start | bytes 24580
  5.6 12.0 %all-to-all-start = ((f32[16,8,256]{2,1,0:T(8,128)}), f32[16,8,256]{2,1,0:T(8,128)S(1)}, u32[]{:S(2)}, u32[]{:S(2)}) async-start(f32[16,8,256]{2,1,0:T(8,128)} %bitcast.65), calls=%async_computation | async-start | bytes 262144 | tf_op jit(solution)/shard_map/all_to_all | solution.py:290
  11.2 3.9 %collective-permute-start = (bf16[16,256]{1,0:T(8,128)(2,1)S(1)}, bf16[16,256]{1,0:T(8,128)(2,1)S(1)}, u32[]{:S(2)}, u32[]{:S(2)}) collective-permute-start(bf16[16,256]{1,0:T(8,128)(2,1)S(1)} %copy-done.1), channel_id=1, source_target_pairs={{0,2},{2,0},{1,3},{3,1},{4,6},{6,4},{5,7},{7,5},{8,10},{10,8},{9,1... | collective-permute-start | bytes 24584 | tf_op jit(solution)/shard_map/ppermute | solution.py:300
  33.2 60.3 %all-to-all-start.2 = ((bf16[8,8,288,128]{3,2,1,0:T(8,128)(2,1)}), bf16[8,8,288,128]{3,2,1,0:T(8,128)(2,1)}, u32[]{:S(2)}, u32[]{:S(2)}) async-start(bf16[8,8,288,128]{3,2,1,0:T(8,128)(2,1)} %bitcast.56), calls=%async_computation.2 | async-start | bytes 9437184 | tf_op jit(solution)/shard_map/all_to_all | solution.py:290
  37.8 1.3 collective-permute-start.5
  39.1 4.0 %collective-permute-start.6 = (bf16[64,256]{1,0:T(8,128)(2,1)S(1)}, bf16[64,256]{1,0:T(8,128)(2,1)S(1)}, u32[]{:S(2)}, u32[]{:S(2)}) collective-permute-start(bf16[64,256]{1,0:T(8,128)(2,1)S(1)} %bitcast.67), channel_id=1, source_target_pairs={{0,12},{4,0},{8,4},{12,8},{1,13},{5,1},{9,5},{13,9},{2,14},{6,2},{... | collective-permute-start | bytes 98312 | tf_op jit(solution)/shard_map/ppermute | solution.py:300
  40.2 5.5 %collective-permute-start.7 = (bf16[64,256]{1,0:T(8,128)(2,1)S(1)}, bf16[64,256]{1,0:T(8,128)(2,1)S(1)}, u32[]{:S(2)}, u32[]{:S(2)}) collective-permute-start(bf16[64,256]{1,0:T(8,128)(2,1)S(1)} %bitcast.68), channel_id=1, source_target_pairs={{0,8},{4,12},{8,0},{12,4},{1,9},{5,13},{9,1},{13,5},{2,10},{6,14},... | collective-permute-start | bytes 98312 | tf_op jit(solution)/shard_map/ppermute | solution.py:300
  41.5 5.1 %collective-permute-start.8 = (bf16[64,256]{1,0:T(8,128)(2,1)S(1)}, bf16[64,256]{1,0:T(8,128)(2,1)S(1)}, u32[]{:S(2)}, u32[]{:S(2)}) collective-permute-start(bf16[64,256]{1,0:T(8,128)(2,1)S(1)} %bitcast.69), channel_id=1, source_target_pairs={{0,4},{4,8},{8,12},{12,0},{1,5},{5,9},{9,13},{13,1},{2,6},{6,10},{... | collective-permute-start | bytes 98312 | tf_op jit(solution)/shard_map/ppermute | solution.py:300
  46.7 5.7 %collective-permute-start.1 = (f32[128,256]{1,0:T(8,128)S(1)}, f32[128,256]{1,0:T(8,128)S(1)}, u32[]{:S(2)}, u32[]{:S(2)}) collective-permute-start(f32[128,256]{1,0:T(8,128)S(1)} %bitcast.59), channel_id=1, source_target_pairs={{0,12},{4,0},{8,4},{12,8},{1,13},{5,1},{9,5},{13,9},{2,14},{6,2},{... | collective-permute-start | bytes 393224 | tf_op jit(solution)/shard_map/ppermute | solution.py:300
  47.9 7.1 %collective-permute-start.2 = (f32[128,256]{1,0:T(8,128)S(1)}, f32[128,256]{1,0:T(8,128)S(1)}, u32[]{:S(2)}, u32[]{:S(2)}) collective-permute-start(f32[128,256]{1,0:T(8,128)S(1)} %bitcast.60), channel_id=1, source_target_pairs={{0,8},{4,12},{8,0},{12,4},{1,9},{5,13},{9,1},{13,5},{2,10},{6,14},... | collective-permute-start | bytes 393224 | tf_op jit(solution)/shard_map/ppermute | solution.py:300
  48.8 7.5 %collective-permute-start.3 = (f32[128,256]{1,0:T(8,128)S(1)}, f32[128,256]{1,0:T(8,128)S(1)}, u32[]{:S(2)}, u32[]{:S(2)}) collective-permute-start(f32[128,256]{1,0:T(8,128)S(1)} %bitcast.61), channel_id=1, source_target_pairs={{0,4},{4,8},{8,12},{12,0},{1,5},{5,9},{9,13},{13,1},{2,6},{6,10},{... | collective-permute-start | bytes 393224 | tf_op jit(solution)/shard_map/ppermute | solution.py:300
  56.4 2.0 %collective-permute-start.4 = (f32[512,256]{1,0:T(8,128)S(1)}, f32[512,256]{1,0:T(8,128)S(1)}, u32[]{:S(2)}, u32[]{:S(2)}) collective-permute-start(f32[512,256]{1,0:T(8,128)S(1)} %bitcast.57), channel_id=1, source_target_pairs={{0,1},{1,0},{2,3},{3,2},{4,5},{5,4},{6,7},{7,6},{8,9},{9,8},{10,11... | collective-permute-start | bytes 1572872 | tf_op jit(solution)/shard_map/ppermute | solution.py:300
  56.6 37.0 %copy-start = (bf16[288,256]{1,0:T(8,128)(2,1)S(1)}, bf16[288,256]{1,0:T(8,128)(2,1)}, u32[]{:S(2)}) copy-start(bf16[288,256]{1,0:T(8,128)(2,1)} %plane_ref.1) | copy-start | bytes 442372
  130.6 2.3 %collective-permute-start.9 = (bf16[1024,256]{1,0:T(8,128)(2,1)S(1)}, bf16[1024,256]{1,0:T(8,128)(2,1)S(1)}, u32[]{:S(2)}, u32[]{:S(2)}) collective-permute-start(bf16[1024,256]{1,0:T(8,128)(2,1)S(1)} %slice.4), channel_id=1, source_target_pairs={{0,1},{1,0},{2,3},{3,2},{4,5},{5,4},{6,7},{7,6},{8,9},{9,8},{10,11... | collective-permute-start | bytes 1572872 | tf_op jit(solution)/shard_map/ppermute | solution.py:300

commit v6 on v5

--- a/solution.py
+++ b/solution.py
@@ -31,7 +31,7 @@
     return mm(a[0], b[0], dims) + (mm(a[0], b[1], dims) + mm(a[1], b[0], dims))
 
 
-def inverse_factor(s, basis_ref, a_ref, m_ref, turned):
+def inverse_factor(s, gram, basis_ref, a_ref, m_ref, turned):
     n = s.shape[1]
     row = lax.broadcasted_iota(jnp.int32, (n, n), 0)
     col = lax.broadcasted_iota(jnp.int32, (n, n), 1)
@@ -45,7 +45,6 @@
         inverse = halves_of(inverse)
         basis_ref[...] = low(fine(inverse, sketch, NT) if turned else fine(sketch, inverse, NT))
 
-    gram = mm(s, s, TN, HIGH)
     on_diag = jnp.where(eye, gram, 0.0)
     inv_row = 0.9 * lax.rsqrt(jnp.sum(on_diag, axis=0, keepdims=True))
     inv_col = 0.9 * lax.rsqrt(jnp.sum(on_diag, axis=1, keepdims=True))
@@ -111,7 +110,7 @@
         for c in range(2)
     ]
     s = jnp.concatenate([s_ref[place * 8 : place * 8 + 8] for place in places], axis=0)
-    inverse_factor(s, basis_ref, a_ref, m_ref, False)
+    inverse_factor(s, mm(s, s, TN, HIGH), basis_ref, a_ref, m_ref, False)
 
 
 def first_basis(sketch):
@@ -130,8 +129,11 @@
 
 def second_core_kernel(got_ref, other_ref, core_ref, basis_ref, a_ref, m_ref):
     lanes = core_ref.shape[1]
-    sketch = got_ref[:, lanes:].astype(jnp.float32) + other_ref[...].astype(jnp.float32)
-    inverse_factor(sketch, basis_ref, a_ref, m_ref, True)
+    here, there = got_ref[:, lanes:], other_ref[...]
+    sketch = here.astype(jnp.float32) + there.astype(jnp.float32)
+    cross = mm(here, there, TN)
+    gram = mm(here, here, TN) + (cross + cross.T) + mm(there, there, TN)
+    inverse_factor(sketch, gram, basis_ref, a_ref, m_ref, True)
     core_ref[...] = mm(basis_ref[...], got_ref[:, :lanes]).astype(core_ref.dtype)
 
 
@@ -174,7 +176,7 @@
 def first_sums(tensor, omega_two, omega_three):
     rows, cols, planes = tensor.shape
     rank = omega_two.shape[1]
-    count = 16
+    count = 32
     return pl.pallas_call(
         first_sums_kernel,
         grid=(rows // count,),
@@ -201,13 +203,18 @@
     basis = basis_ref[...]
     weight = plane_ref[...].astype(jnp.float32)
     sketch = []
-    for j in range(rows):
-        loads[j].wait()
-        slab = jnp.concatenate([slab_ref[j, b] for b in range(slab_ref.shape[1])], axis=1)
-        core = mm(slab, basis)
-        core_ref[j] = low(core.T)
-        inner = mm(low(core), rank_ref[...])
-        sketch.append(jnp.sum(inner * weight, axis=0, keepdims=True))
+    batch = 4
+    for first in range(0, rows, batch):
+        slabs = []
+        for j in range(first, first + batch):
+            loads[j].wait()
+            slabs.append(jnp.concatenate([slab_ref[j, b] for b in range(slab_ref.shape[1])], axis=1))
+        cores = mm(jnp.concatenate(slabs, axis=0), basis)
+        inners = mm(low(cores), rank_ref[...])
+        for at in range(batch):
+            here = slice(at * planes, (at + 1) * planes)
+            core_ref[first + at] = low(cores[here].T)
+            sketch.append(jnp.sum(inners[here] * weight, axis=0, keepdims=True))
     sketch = jnp.concatenate(sketch, axis=0)
     upper = low(sketch)
     lower = low(sketch - upper.astype(jnp.float32))

time: 153 us -> 150 us (0.980)
  Pallas kernels: 24.1 us -> 21.3 us
where the time goes in v6:
time: 150 us
  blocking collectives  59.3 us (40%)
  waiting for transfers between devices  50.6 us (34%)
  Pallas kernels  21.3 us (14%)
  starting transfers between devices  18.2 us (12%)
    all_to_all x3, blocking collectives, exchange(): return lax.all_to_all(blocks, axes, split_axis=0, concat_axis=0, tiled=True)  59.3 us
    all_to_all x2, waiting for transfers between devices, exchange(): return lax.all_to_all(blocks, axes, split_axis=0, concat_axis=0, tiled=True)  32.2 us
    ppermute x10, waiting for transfers between devices, around(): lax.ppermute(block, axes, [(p, (p + step) % count) for p in range(count)])  18.4 us
    all_to_all x2, starting transfers between devices, exchange(): return lax.all_to_all(blocks, axes, split_axis=0, concat_axis=0, tiled=True)  10.1 us
    ppermute x10, starting transfers between devices, around(): lax.ppermute(block, axes, [(p, (p + step) % count) for p in range(count)])  8.12 us
    pallas_call x1, Pallas kernels, project(): pl.pallas_call(project_kernel, out_shape=jax.ShapeDtypeStruct((rank // 2...  5.55 us
    pallas_call x1, Pallas kernels, first_basis(): pl.pallas_call(first_basis_kernel, out_shape=jax.ShapeDtypeStruct(sketch....  5.16 us
    pallas_call x1, Pallas kernels, first_sums(): pl.pallas_call(first_sums_kernel, grid=(rows // count,), out_shape=jax.Sh...  4.99 us
  transfers between devices with their start and end apart: 12, of which 12 were waited for; matrix products, arithmetic and copies ran while one was open for 0% of the time, Pallas kernels for 3%

profile of v6, /device:TPU:0, one launch (start us, length us, event | category | flops | bytes accessed | tf_op | source)
XLA Modules:
  0.0 150.1 jit_solution(376549128052828923)
XLA Ops:
  0.0 5.0 %first_sums.1 = f32[128,256]{1,0:T(8,128)} custom-call(bf16[64,256]{1,0:T(8,128)(2,1)} %two_ref.1, bf16[288,256]{1,0:T(8,128)(2,1)} %three_ref.1, bf16[64,288,128]{2,1,0:T(8,128)(2,1)} %bitcast.55), custom_call_target="tpu_custom_call" | custom-call | flops 1000000000 | bytes 5000000 | tf_op jit(solution)/shard_map/first_sums/pallas_call | solution.py:180
  5.0 5.5 %all-to-all-start = ((f32[16,8,256]{2,1,0:T(8,128)}), f32[16,8,256]{2,1,0:T(8,128)S(1)}, u32[]{:S(2)}, u32[]{:S(2)}) async-start(f32[16,8,256]{2,1,0:T(8,128)} %bitcast.65), calls=%async_computation | async-start | bytes 262144 | tf_op jit(solution)/shard_map/all_to_all | solution.py:297
  10.5 2.0 %collective-permute-start = (bf16[16,256]{1,0:T(8,128)(2,1)S(1)}, bf16[16,256]{1,0:T(8,128)(2,1)S(1)}, u32[]{:S(2)}, u32[]{:S(2)}) collective-permute-start(bf16[16,256]{1,0:T(8,128)(2,1)S(1)} %copy-done.1), channel_id=1, source_target_pairs={{0,2},{2,0},{1,3},{3,1},{4,6},{6,4},{5,7},{7,5},{8,10},{10,8},{9,1... | collective-permute-start | bytes 24584 | tf_op jit(solution)/shard_map/ppermute | solution.py:307
  12.5 1.9 %collective-permute-done = bf16[16,256]{1,0:T(8,128)(2,1)S(1)} collective-permute-done((bf16[16,256]{1,0:T(8,128)(2,1)S(1)}, bf16[16,256]{1,0:T(8,128)(2,1)S(1)}, u32[]{:S(2)}, u32[]{:S(2)}) %collective-permute-start) | collective-permute-done | bytes 8224 | tf_op jit(solution)/shard_map/ppermute | solution.py:307
  14.5 2.5 %all-to-all-done = f32[16,8,256]{2,1,0:T(8,128)S(1)} async-done(((f32[16,8,256]{2,1,0:T(8,128)}), f32[16,8,256]{2,1,0:T(8,128)S(1)}, u32[]{:S(2)}, u32[]{:S(2)}) %all-to-all-start) | async-done | bytes 131104 | tf_op jit(solution)/shard_map/all_to_all | solution.py:297
  17.0 15.5 %all_to_all.25 = f32[16,8,256]{2,1,0:T(8,128)S(1)} all-to-all(f32[16,8,256]{2,1,0:T(8,128)S(1)} %broadcast_in_dim.2), channel_id=1, replica_groups=mesh['z'=4,'yh'=2,'x'=4,'yl'=2,'c'=2] {'z','yh','yl'}, dimensions={0} | all-to-all | bytes 262144 | tf_op jit(solution)/shard_map/all_to_all | solution.py:297
  32.5 4.6 %all-to-all-start.2 = ((bf16[8,8,288,128]{3,2,1,0:T(8,128)(2,1)}), bf16[8,8,288,128]{3,2,1,0:T(8,128)(2,1)}, u32[]{:S(2)}, u32[]{:S(2)}) async-start(bf16[8,8,288,128]{3,2,1,0:T(8,128)(2,1)} %bitcast.56), calls=%async_computation.2 | async-start | bytes 9437184 | tf_op jit(solution)/shard_map/all_to_all | solution.py:297
  37.2 0.1 collective-permute-start.5
  37.2 1.2 collective-permute-done.5
  38.5 1.1 collective-permute-start.6
  39.6 1.3 collective-permute-start.7
  40.9 0.3 collective-permute-start.8
  41.2 1.3 collective-permute-done.6
  42.4 2.7 %collective-permute-done.7 = bf16[64,256]{1,0:T(8,128)(2,1)S(1)} collective-permute-done((bf16[64,256]{1,0:T(8,128)(2,1)S(1)}, bf16[64,256]{1,0:T(8,128)(2,1)S(1)}, u32[]{:S(2)}, u32[]{:S(2)}) %collective-permute-start.7) | collective-permute-done | bytes 32800 | tf_op jit(solution)/shard_map/ppermute | solution.py:307
  45.1 0.9 collective-permute-done.8
  46.0 1.2 collective-permute-start.1
  47.2 0.9 collective-permute-start.2
  48.1 0.4 collective-permute-start.3
  48.5 3.2 %collective-permute-done.1 = f32[128,256]{1,0:T(8,128)S(1)} collective-permute-done((f32[128,256]{1,0:T(8,128)S(1)}, f32[128,256]{1,0:T(8,128)S(1)}, u32[]{:S(2)}, u32[]{:S(2)}) %collective-permute-start.1) | collective-permute-done | bytes 131104 | tf_op jit(solution)/shard_map/ppermute | solution.py:307
  51.8 2.5 %collective-permute-done.2 = f32[128,256]{1,0:T(8,128)S(1)} collective-permute-done((f32[128,256]{1,0:T(8,128)S(1)}, f32[128,256]{1,0:T(8,128)S(1)}, u32[]{:S(2)}, u32[]{:S(2)}) %collective-permute-start.2) | collective-permute-done | bytes 131104 | tf_op jit(solution)/shard_map/ppermute | solution.py:307
  54.3 1.3 collective-permute-done.3
  56.0 1.8 %collective-permute-done.4 = f32[512,256]{1,0:T(8,128)S(1)} collective-permute-done((f32[512,256]{1,0:T(8,128)S(1)}, f32[512,256]{1,0:T(8,128)S(1)}, u32[]{:S(2)}, u32[]{:S(2)}) %collective-permute-start.4) | collective-permute-done | bytes 524320 | tf_op jit(solution)/shard_map/ppermute | solution.py:307
  57.8 0.2 fusion.2
  58.0 5.2 %first_basis.1.basis_ref = bf16[1024,256]{1,0:T(8,128)(2,1)S(1)} custom-call(f32[1024,256]{1,0:T(8,128)S(1)} %bitcast.49), custom_call_target="tpu_custom_call" | custom-call | tf_op jit(solution)/shard_map/first_basis/pallas_call | solution.py:118
  63.2 29.7 %all-to-all-done.2.moved_ref = bf16[8,8,288,128]{3,2,1,0:T(8,128)(2,1)} async-done(((bf16[8,8,288,128]{3,2,1,0:T(8,128)(2,1)}), bf16[8,8,288,128]{3,2,1,0:T(8,128)(2,1)}, u32[]{:S(2)}, u32[]{:S(2)}) %all-to-all-start.2) | async-done | bytes 4718624 | tf_op jit(solution)/shard_map/all_to_all | solution.py:297
  92.9 5.6 %project.1 = bf16[1024,896]{1,0:T(8,128)(2,1)S(1)} custom-call(bf16[1024,256]{1,0:T(8,128)(2,1)S(1)} %first_basis.1.basis_ref, bf16[288,256]{1,0:T(8,128)(2,1)S(1)} %copy-done, bf16[256,256]{1,0:T(8,128)(2,1)S(1)} %bitcast.54, bf16[8,8,288,128]{3,2,1,0:T(8,128)(2,1)} %all-to-all-done.2.moved_ref), custom_call_target="tpu_custom_call" | custom-call | flops 2000000000 | bytes 8000000 | tf_op jit(solution)/shard_map/project/pallas_call | solution.py:245
  98.4 30.5 %all_to_all.26 = bf16[128,8,896]{2,1,0:T(8,128)(2,1)S(1)} all-to-all(bf16[128,8,896]{2,1,0:T(8,128)(2,1)S(1)} %bitcast.52), channel_id=1, replica_groups=mesh['z'=4,'yh'=2,'x'=4,'yl'=2,'c'=2] {'x','yl','c','z','yh'}, dimensions={0} | all-to-all | bytes 3670016 | tf_op jit(solution)/shard_map/all_to_all | solution.py:297
  129.0 0.8 collective-permute-start.9
  129.8 1.5 %collective-permute-done.9.other_ref = bf16[1024,256]{1,0:T(8,128)(2,1)S(1)} collective-permute-done((bf16[1024,256]{1,0:T(8,128)(2,1)S(1)}, bf16[1024,256]{1,0:T(8,128)(2,1)S(1)}, u32[]{:S(2)}, u32[]{:S(2)}) %collective-permute-start.9) | collective-permute-done | bytes 524320 | tf_op jit(solution)/shard_map/ppermute | solution.py:307
  131.3 4.4 %second_core.1 = bf16[256,640]{1,0:T(8,128)(2,1)S(1)} custom-call(bf16[1024,896]{1,0:T(8,128)(2,1)S(1)} %bitcast.51, bf16[1024,256]{1,0:T(8,128)(2,1)S(1)} %collective-permute-done.9.other_ref), custom_call_target="tpu_custom_call" | custom-call | flops 4000000000 | bytes 3000000 | tf_op jit(solution)/shard_map/second_core/pallas_call | solution.py:143
  135.7 13.2 %all_to_all.27.got_ref = bf16[8,32,640]{2,1,0:T(8,128)(2,1)S(1)} all-to-all(bf16[8,32,640]{2,1,0:T(8,128)(2,1)S(1)} %bitcast.53), channel_id=1, replica_groups=mesh['z'=4,'yh'=2,'x'=4,'yl'=2,'c'=2] {'z','yh'}, dimensions={0} | all-to-all | bytes 655360 | tf_op jit(solution)/shard_map/all_to_all | solution.py:297
  148.9 1.2 merge.1
  (29 shorter events, 0.4 us)
Async XLA Ops:
  0.0 10.5 %copy-start.1 = (bf16[16,256]{1,0:T(8,128)(2,1)S(1)}, bf16[16,256]{1,0:T(8,128)(2,1)}, u32[]{:S(2)}) copy-start(bf16[16,256]{1,0:T(8,128)(2,1)} %param.8) | copy-start | bytes 24580
  5.0 12.0 %all-to-all-start = ((f32[16,8,256]{2,1,0:T(8,128)}), f32[16,8,256]{2,1,0:T(8,128)S(1)}, u32[]{:S(2)}, u32[]{:S(2)}) async-start(f32[16,8,256]{2,1,0:T(8,128)} %bitcast.65), calls=%async_computation | async-start | bytes 262144 | tf_op jit(solution)/shard_map/all_to_all | solution.py:297
  10.5 3.9 %collective-permute-start = (bf16[16,256]{1,0:T(8,128)(2,1)S(1)}, bf16[16,256]{1,0:T(8,128)(2,1)S(1)}, u32[]{:S(2)}, u32[]{:S(2)}) collective-permute-start(bf16[16,256]{1,0:T(8,128)(2,1)S(1)} %copy-done.1), channel_id=1, source_target_pairs={{0,2},{2,0},{1,3},{3,1},{4,6},{6,4},{5,7},{7,5},{8,10},{10,8},{9,1... | collective-permute-start | bytes 24584 | tf_op jit(solution)/shard_map/ppermute | solution.py:307
  32.5 60.3 %all-to-all-start.2 = ((bf16[8,8,288,128]{3,2,1,0:T(8,128)(2,1)}), bf16[8,8,288,128]{3,2,1,0:T(8,128)(2,1)}, u32[]{:S(2)}, u32[]{:S(2)}) async-start(bf16[8,8,288,128]{3,2,1,0:T(8,128)(2,1)} %bitcast.56), calls=%async_computation.2 | async-start | bytes 9437184 | tf_op jit(solution)/shard_map/all_to_all | solution.py:297
  37.2 1.3 collective-permute-start.5
  38.5 4.0 %collective-permute-start.6 = (bf16[64,256]{1,0:T(8,128)(2,1)S(1)}, bf16[64,256]{1,0:T(8,128)(2,1)S(1)}, u32[]{:S(2)}, u32[]{:S(2)}) collective-permute-start(bf16[64,256]{1,0:T(8,128)(2,1)S(1)} %bitcast.67), channel_id=1, source_target_pairs={{0,12},{4,0},{8,4},{12,8},{1,13},{5,1},{9,5},{13,9},{2,14},{6,2},{... | collective-permute-start | bytes 98312 | tf_op jit(solution)/shard_map/ppermute | solution.py:307
  39.6 5.5 %collective-permute-start.7 = (bf16[64,256]{1,0:T(8,128)(2,1)S(1)}, bf16[64,256]{1,0:T(8,128)(2,1)S(1)}, u32[]{:S(2)}, u32[]{:S(2)}) collective-permute-start(bf16[64,256]{1,0:T(8,128)(2,1)S(1)} %bitcast.68), channel_id=1, source_target_pairs={{0,8},{4,12},{8,0},{12,4},{1,9},{5,13},{9,1},{13,5},{2,10},{6,14},... | collective-permute-start | bytes 98312 | tf_op jit(solution)/shard_map/ppermute | solution.py:307
  40.9 5.1 %collective-permute-start.8 = (bf16[64,256]{1,0:T(8,128)(2,1)S(1)}, bf16[64,256]{1,0:T(8,128)(2,1)S(1)}, u32[]{:S(2)}, u32[]{:S(2)}) collective-permute-start(bf16[64,256]{1,0:T(8,128)(2,1)S(1)} %bitcast.69), channel_id=1, source_target_pairs={{0,4},{4,8},{8,12},{12,0},{1,5},{5,9},{9,13},{13,1},{2,6},{6,10},{... | collective-permute-start | bytes 98312 | tf_op jit(solution)/shard_map/ppermute | solution.py:307
  46.0 5.7 %collective-permute-start.1 = (f32[128,256]{1,0:T(8,128)S(1)}, f32[128,256]{1,0:T(8,128)S(1)}, u32[]{:S(2)}, u32[]{:S(2)}) collective-permute-start(f32[128,256]{1,0:T(8,128)S(1)} %bitcast.59), channel_id=1, source_target_pairs={{0,12},{4,0},{8,4},{12,8},{1,13},{5,1},{9,5},{13,9},{2,14},{6,2},{... | collective-permute-start | bytes 393224 | tf_op jit(solution)/shard_map/ppermute | solution.py:307
  47.2 7.1 %collective-permute-start.2 = (f32[128,256]{1,0:T(8,128)S(1)}, f32[128,256]{1,0:T(8,128)S(1)}, u32[]{:S(2)}, u32[]{:S(2)}) collective-permute-start(f32[128,256]{1,0:T(8,128)S(1)} %bitcast.60), channel_id=1, source_target_pairs={{0,8},{4,12},{8,0},{12,4},{1,9},{5,13},{9,1},{13,5},{2,10},{6,14},... | collective-permute-start | bytes 393224 | tf_op jit(solution)/shard_map/ppermute | solution.py:307
  48.1 7.5 %collective-permute-start.3 = (f32[128,256]{1,0:T(8,128)S(1)}, f32[128,256]{1,0:T(8,128)S(1)}, u32[]{:S(2)}, u32[]{:S(2)}) collective-permute-start(f32[128,256]{1,0:T(8,128)S(1)} %bitcast.61), channel_id=1, source_target_pairs={{0,4},{4,8},{8,12},{12,0},{1,5},{5,9},{9,13},{13,1},{2,6},{6,10},{... | collective-permute-start | bytes 393224 | tf_op jit(solution)/shard_map/ppermute | solution.py:307
  55.8 2.0 %collective-permute-start.4 = (f32[512,256]{1,0:T(8,128)S(1)}, f32[512,256]{1,0:T(8,128)S(1)}, u32[]{:S(2)}, u32[]{:S(2)}) collective-permute-start(f32[512,256]{1,0:T(8,128)S(1)} %bitcast.57), channel_id=1, source_target_pairs={{0,1},{1,0},{2,3},{3,2},{4,5},{5,4},{6,7},{7,6},{8,9},{9,8},{10,11... | collective-permute-start | bytes 1572872 | tf_op jit(solution)/shard_map/ppermute | solution.py:307
  55.9 37.0 %copy-start = (bf16[288,256]{1,0:T(8,128)(2,1)S(1)}, bf16[288,256]{1,0:T(8,128)(2,1)}, u32[]{:S(2)}) copy-start(bf16[288,256]{1,0:T(8,128)(2,1)} %plane_ref.1) | copy-start | bytes 442372
  129.0 2.3 %collective-permute-start.9 = (bf16[1024,256]{1,0:T(8,128)(2,1)S(1)}, bf16[1024,256]{1,0:T(8,128)(2,1)S(1)}, u32[]{:S(2)}, u32[]{:S(2)}) collective-permute-start(bf16[1024,256]{1,0:T(8,128)(2,1)S(1)} %slice.4), channel_id=1, source_target_pairs={{0,1},{1,0},{2,3},{3,2},{4,5},{5,4},{6,7},{7,6},{8,9},{9,8},{10,11... | collective-permute-start | bytes 1572872 | tf_op jit(solution)/shard_map/ppermute | solution.py:307

commit v7 on v6

--- a/solution.py
+++ b/solution.py
@@ -159,10 +159,15 @@
     weight = two_ref[pl.ds(pl.multiple_of(step * count, count), count), :]
     weight = weight.astype(jnp.float32)
     total = None
-    for j in range(count):
-        inner = mm(slabs_ref[j], three_ref[...], TN)
-        term = inner * weight[j : j + 1]
-        total = term if total is None else total + term
+    batch = 4
+    cols = slabs_ref.shape[2]
+    for first in range(0, count, batch):
+        slabs = jnp.concatenate([slabs_ref[first + at] for at in range(batch)], axis=1)
+        inner = mm(slabs, three_ref[...], TN)
+        for at in range(batch):
+            j = first + at
+            term = inner[at * cols : (at + 1) * cols] * weight[j : j + 1]
+            total = term if total is None else total + term
 
     @pl.when(step == 0)
     def _():
@@ -203,7 +208,7 @@
     basis = basis_ref[...]
     weight = plane_ref[...].astype(jnp.float32)
     sketch = []
-    batch = 4
+    batch = 2
     for first in range(0, rows, batch):
         slabs = []
         for j in range(first, first + batch):

time: 150 us -> 151 us (level)
  no operation moved by 1% of the time
where the time goes in v7:
time: 151 us; the launch traced here: 150 us
  blocking collectives  59.3 us (39%)
  waiting for transfers between devices  50.6 us (34%)
  Pallas kernels  21.5 us (14%)
  starting transfers between devices  18.2 us (12%)
    all_to_all x3, blocking collectives, exchange(): return lax.all_to_all(blocks, axes, split_axis=0, concat_axis=0, tiled=True)  59.3 us
    all_to_all x2, waiting for transfers between devices, exchange(): return lax.all_to_all(blocks, axes, split_axis=0, concat_axis=0, tiled=True)  32.2 us
    ppermute x10, waiting for transfers between devices, around(): lax.ppermute(block, axes, [(p, (p + step) % count) for p in range(count)])  18.4 us
    all_to_all x2, starting transfers between devices, exchange(): return lax.all_to_all(blocks, axes, split_axis=0, concat_axis=0, tiled=True)  10.1 us
    ppermute x10, starting transfers between devices, around(): lax.ppermute(block, axes, [(p, (p + step) % count) for p in range(count)])  8.12 us
    pallas_call x1, Pallas kernels, project(): pl.pallas_call(project_kernel, out_shape=jax.ShapeDtypeStruct((rank // 2...  5.72 us
    pallas_call x1, Pallas kernels, first_basis(): pl.pallas_call(first_basis_kernel, out_shape=jax.ShapeDtypeStruct(sketch....  5.17 us
    pallas_call x1, Pallas kernels, first_sums(): pl.pallas_call(first_sums_kernel, grid=(rows // count,), out_shape=jax.Sh...  5 us
  transfers between devices with their start and end apart: 12, of which 12 were waited for; matrix products, arithmetic and copies ran while one was open for 0% of the time, Pallas kernels for 3%

profile of v7, /device:TPU:0, one launch (start us, length us, event | category | flops | bytes accessed | tf_op | source)
XLA Modules:
  0.0 150.3 jit_solution(10194215394096963807)
XLA Ops:
  0.0 5.0 %first_sums.1 = f32[128,256]{1,0:T(8,128)} custom-call(bf16[64,256]{1,0:T(8,128)(2,1)} %two_ref.1, bf16[288,256]{1,0:T(8,128)(2,1)} %three_ref.1, bf16[64,288,128]{2,1,0:T(8,128)(2,1)} %bitcast.55), custom_call_target="tpu_custom_call" | custom-call | flops 1000000000 | bytes 5000000 | tf_op jit(solution)/shard_map/first_sums/pallas_call | solution.py:185
  5.0 5.5 %all-to-all-start = ((f32[16,8,256]{2,1,0:T(8,128)}), f32[16,8,256]{2,1,0:T(8,128)S(1)}, u32[]{:S(2)}, u32[]{:S(2)}) async-start(f32[16,8,256]{2,1,0:T(8,128)} %bitcast.65), calls=%async_computation | async-start | bytes 262144 | tf_op jit(solution)/shard_map/all_to_all | solution.py:302
  10.5 2.0 %collective-permute-start = (bf16[16,256]{1,0:T(8,128)(2,1)S(1)}, bf16[16,256]{1,0:T(8,128)(2,1)S(1)}, u32[]{:S(2)}, u32[]{:S(2)}) collective-permute-start(bf16[16,256]{1,0:T(8,128)(2,1)S(1)} %copy-done.1), channel_id=1, source_target_pairs={{0,2},{2,0},{1,3},{3,1},{4,6},{6,4},{5,7},{7,5},{8,10},{10,8},{9,1... | collective-permute-start | bytes 24584 | tf_op jit(solution)/shard_map/ppermute | solution.py:312
  12.5 1.9 %collective-permute-done = bf16[16,256]{1,0:T(8,128)(2,1)S(1)} collective-permute-done((bf16[16,256]{1,0:T(8,128)(2,1)S(1)}, bf16[16,256]{1,0:T(8,128)(2,1)S(1)}, u32[]{:S(2)}, u32[]{:S(2)}) %collective-permute-start) | collective-permute-done | bytes 8224 | tf_op jit(solution)/shard_map/ppermute | solution.py:312
  14.5 2.5 %all-to-all-done = f32[16,8,256]{2,1,0:T(8,128)S(1)} async-done(((f32[16,8,256]{2,1,0:T(8,128)}), f32[16,8,256]{2,1,0:T(8,128)S(1)}, u32[]{:S(2)}, u32[]{:S(2)}) %all-to-all-start) | async-done | bytes 131104 | tf_op jit(solution)/shard_map/all_to_all | solution.py:302
  17.0 15.5 %all_to_all.25 = f32[16,8,256]{2,1,0:T(8,128)S(1)} all-to-all(f32[16,8,256]{2,1,0:T(8,128)S(1)} %broadcast_in_dim.2), channel_id=1, replica_groups=mesh['z'=4,'yh'=2,'x'=4,'yl'=2,'c'=2] {'z','yh','yl'}, dimensions={0} | all-to-all | bytes 262144 | tf_op jit(solution)/shard_map/all_to_all | solution.py:302
  32.6 4.6 %all-to-all-start.2 = ((bf16[8,8,288,128]{3,2,1,0:T(8,128)(2,1)}), bf16[8,8,288,128]{3,2,1,0:T(8,128)(2,1)}, u32[]{:S(2)}, u32[]{:S(2)}) async-start(bf16[8,8,288,128]{3,2,1,0:T(8,128)(2,1)} %bitcast.56), calls=%async_computation.2 | async-start | bytes 9437184 | tf_op jit(solution)/shard_map/all_to_all | solution.py:302
  37.2 0.1 collective-permute-start.5
  37.3 1.2 collective-permute-done.5
  38.5 1.1 collective-permute-start.6
  39.6 1.3 collective-permute-start.7
  40.9 0.3 collective-permute-start.8
  41.2 1.3 collective-permute-done.6
  42.4 2.7 %collective-permute-done.7 = bf16[64,256]{1,0:T(8,128)(2,1)S(1)} collective-permute-done((bf16[64,256]{1,0:T(8,128)(2,1)S(1)}, bf16[64,256]{1,0:T(8,128)(2,1)S(1)}, u32[]{:S(2)}, u32[]{:S(2)}) %collective-permute-start.7) | collective-permute-done | bytes 32800 | tf_op jit(solution)/shard_map/ppermute | solution.py:312
  45.1 0.9 collective-permute-done.8
  46.0 1.2 collective-permute-start.1
  47.2 0.9 collective-permute-start.2
  48.1 0.4 collective-permute-start.3
  48.5 3.2 %collective-permute-done.1 = f32[128,256]{1,0:T(8,128)S(1)} collective-permute-done((f32[128,256]{1,0:T(8,128)S(1)}, f32[128,256]{1,0:T(8,128)S(1)}, u32[]{:S(2)}, u32[]{:S(2)}) %collective-permute-start.1) | collective-permute-done | bytes 131104 | tf_op jit(solution)/shard_map/ppermute | solution.py:312
  51.8 2.5 %collective-permute-done.2 = f32[128,256]{1,0:T(8,128)S(1)} collective-permute-done((f32[128,256]{1,0:T(8,128)S(1)}, f32[128,256]{1,0:T(8,128)S(1)}, u32[]{:S(2)}, u32[]{:S(2)}) %collective-permute-start.2) | collective-permute-done | bytes 131104 | tf_op jit(solution)/shard_map/ppermute | solution.py:312
  54.3 1.3 collective-permute-done.3
  56.0 1.8 %collective-permute-done.4 = f32[512,256]{1,0:T(8,128)S(1)} collective-permute-done((f32[512,256]{1,0:T(8,128)S(1)}, f32[512,256]{1,0:T(8,128)S(1)}, u32[]{:S(2)}, u32[]{:S(2)}) %collective-permute-start.4) | collective-permute-done | bytes 524320 | tf_op jit(solution)/shard_map/ppermute | solution.py:312
  57.8 0.2 fusion.2
  58.0 5.2 %first_basis.1.basis_ref = bf16[1024,256]{1,0:T(8,128)(2,1)S(1)} custom-call(f32[1024,256]{1,0:T(8,128)S(1)} %bitcast.49), custom_call_target="tpu_custom_call" | custom-call | tf_op jit(solution)/shard_map/first_basis/pallas_call | solution.py:118
  63.2 29.7 %all-to-all-done.2.moved_ref = bf16[8,8,288,128]{3,2,1,0:T(8,128)(2,1)} async-done(((bf16[8,8,288,128]{3,2,1,0:T(8,128)(2,1)}), bf16[8,8,288,128]{3,2,1,0:T(8,128)(2,1)}, u32[]{:S(2)}, u32[]{:S(2)}) %all-to-all-start.2) | async-done | bytes 4718624 | tf_op jit(solution)/shard_map/all_to_all | solution.py:302
  92.9 5.7 %project.1 = bf16[1024,896]{1,0:T(8,128)(2,1)S(1)} custom-call(bf16[1024,256]{1,0:T(8,128)(2,1)S(1)} %first_basis.1.basis_ref, bf16[288,256]{1,0:T(8,128)(2,1)S(1)} %copy-done, bf16[256,256]{1,0:T(8,128)(2,1)S(1)} %bitcast.54, bf16[8,8,288,128]{3,2,1,0:T(8,128)(2,1)} %all-to-all-done.2.moved_ref), custom_call_target="tpu_custom_call" | custom-call | flops 2000000000 | bytes 8000000 | tf_op jit(solution)/shard_map/project/pallas_call | solution.py:250
  98.6 30.5 %all_to_all.26 = bf16[128,8,896]{2,1,0:T(8,128)(2,1)S(1)} all-to-all(bf16[128,8,896]{2,1,0:T(8,128)(2,1)S(1)} %bitcast.52), channel_id=1, replica_groups=mesh['z'=4,'yh'=2,'x'=4,'yl'=2,'c'=2] {'x','yl','c','z','yh'}, dimensions={0} | all-to-all | bytes 3670016 | tf_op jit(solution)/shard_map/all_to_all | solution.py:302
  129.2 0.8 collective-permute-start.9
  129.9 1.5 %collective-permute-done.9.other_ref = bf16[1024,256]{1,0:T(8,128)(2,1)S(1)} collective-permute-done((bf16[1024,256]{1,0:T(8,128)(2,1)S(1)}, bf16[1024,256]{1,0:T(8,128)(2,1)S(1)}, u32[]{:S(2)}, u32[]{:S(2)}) %collective-permute-start.9) | collective-permute-done | bytes 524320 | tf_op jit(solution)/shard_map/ppermute | solution.py:312
  131.5 4.4 %second_core.1 = bf16[256,640]{1,0:T(8,128)(2,1)S(1)} custom-call(bf16[1024,896]{1,0:T(8,128)(2,1)S(1)} %bitcast.51, bf16[1024,256]{1,0:T(8,128)(2,1)S(1)} %collective-permute-done.9.other_ref), custom_call_target="tpu_custom_call" | custom-call | flops 4000000000 | bytes 3000000 | tf_op jit(solution)/shard_map/second_core/pallas_call | solution.py:143
  135.8 13.2 %all_to_all.27.got_ref = bf16[8,32,640]{2,1,0:T(8,128)(2,1)S(1)} all-to-all(bf16[8,32,640]{2,1,0:T(8,128)(2,1)S(1)} %bitcast.53), channel_id=1, replica_groups=mesh['z'=4,'yh'=2,'x'=4,'yl'=2,'c'=2] {'z','yh'}, dimensions={0} | all-to-all | bytes 655360 | tf_op jit(solution)/shard_map/all_to_all | solution.py:302
  149.0 1.2 merge.1
  (29 shorter events, 0.4 us)
Async XLA Ops:
  0.0 10.5 %copy-start.1 = (bf16[16,256]{1,0:T(8,128)(2,1)S(1)}, bf16[16,256]{1,0:T(8,128)(2,1)}, u32[]{:S(2)}) copy-start(bf16[16,256]{1,0:T(8,128)(2,1)} %param.8) | copy-start | bytes 24580
  5.0 12.0 %all-to-all-start = ((f32[16,8,256]{2,1,0:T(8,128)}), f32[16,8,256]{2,1,0:T(8,128)S(1)}, u32[]{:S(2)}, u32[]{:S(2)}) async-start(f32[16,8,256]{2,1,0:T(8,128)} %bitcast.65), calls=%async_computation | async-start | bytes 262144 | tf_op jit(solution)/shard_map/all_to_all | solution.py:302
  10.5 3.9 %collective-permute-start = (bf16[16,256]{1,0:T(8,128)(2,1)S(1)}, bf16[16,256]{1,0:T(8,128)(2,1)S(1)}, u32[]{:S(2)}, u32[]{:S(2)}) collective-permute-start(bf16[16,256]{1,0:T(8,128)(2,1)S(1)} %copy-done.1), channel_id=1, source_target_pairs={{0,2},{2,0},{1,3},{3,1},{4,6},{6,4},{5,7},{7,5},{8,10},{10,8},{9,1... | collective-permute-start | bytes 24584 | tf_op jit(solution)/shard_map/ppermute | solution.py:312
  32.6 60.3 %all-to-all-start.2 = ((bf16[8,8,288,128]{3,2,1,0:T(8,128)(2,1)}), bf16[8,8,288,128]{3,2,1,0:T(8,128)(2,1)}, u32[]{:S(2)}, u32[]{:S(2)}) async-start(bf16[8,8,288,128]{3,2,1,0:T(8,128)(2,1)} %bitcast.56), calls=%async_computation.2 | async-start | bytes 9437184 | tf_op jit(solution)/shard_map/all_to_all | solution.py:302
  37.2 1.3 collective-permute-start.5
  38.5 4.0 %collective-permute-start.6 = (bf16[64,256]{1,0:T(8,128)(2,1)S(1)}, bf16[64,256]{1,0:T(8,128)(2,1)S(1)}, u32[]{:S(2)}, u32[]{:S(2)}) collective-permute-start(bf16[64,256]{1,0:T(8,128)(2,1)S(1)} %bitcast.67), channel_id=1, source_target_pairs={{0,12},{4,0},{8,4},{12,8},{1,13},{5,1},{9,5},{13,9},{2,14},{6,2},{... | collective-permute-start | bytes 98312 | tf_op jit(solution)/shard_map/ppermute | solution.py:312
  39.6 5.5 %collective-permute-start.7 = (bf16[64,256]{1,0:T(8,128)(2,1)S(1)}, bf16[64,256]{1,0:T(8,128)(2,1)S(1)}, u32[]{:S(2)}, u32[]{:S(2)}) collective-permute-start(bf16[64,256]{1,0:T(8,128)(2,1)S(1)} %bitcast.68), channel_id=1, source_target_pairs={{0,8},{4,12},{8,0},{12,4},{1,9},{5,13},{9,1},{13,5},{2,10},{6,14},... | collective-permute-start | bytes 98312 | tf_op jit(solution)/shard_map/ppermute | solution.py:312
  40.9 5.1 %collective-permute-start.8 = (bf16[64,256]{1,0:T(8,128)(2,1)S(1)}, bf16[64,256]{1,0:T(8,128)(2,1)S(1)}, u32[]{:S(2)}, u32[]{:S(2)}) collective-permute-start(bf16[64,256]{1,0:T(8,128)(2,1)S(1)} %bitcast.69), channel_id=1, source_target_pairs={{0,4},{4,8},{8,12},{12,0},{1,5},{5,9},{9,13},{13,1},{2,6},{6,10},{... | collective-permute-start | bytes 98312 | tf_op jit(solution)/shard_map/ppermute | solution.py:312
  46.0 5.7 %collective-permute-start.1 = (f32[128,256]{1,0:T(8,128)S(1)}, f32[128,256]{1,0:T(8,128)S(1)}, u32[]{:S(2)}, u32[]{:S(2)}) collective-permute-start(f32[128,256]{1,0:T(8,128)S(1)} %bitcast.59), channel_id=1, source_target_pairs={{0,12},{4,0},{8,4},{12,8},{1,13},{5,1},{9,5},{13,9},{2,14},{6,2},{... | collective-permute-start | bytes 393224 | tf_op jit(solution)/shard_map/ppermute | solution.py:312
  47.2 7.1 %collective-permute-start.2 = (f32[128,256]{1,0:T(8,128)S(1)}, f32[128,256]{1,0:T(8,128)S(1)}, u32[]{:S(2)}, u32[]{:S(2)}) collective-permute-start(f32[128,256]{1,0:T(8,128)S(1)} %bitcast.60), channel_id=1, source_target_pairs={{0,8},{4,12},{8,0},{12,4},{1,9},{5,13},{9,1},{13,5},{2,10},{6,14},... | collective-permute-start | bytes 393224 | tf_op jit(solution)/shard_map/ppermute | solution.py:312
  48.1 7.5 %collective-permute-start.3 = (f32[128,256]{1,0:T(8,128)S(1)}, f32[128,256]{1,0:T(8,128)S(1)}, u32[]{:S(2)}, u32[]{:S(2)}) collective-permute-start(f32[128,256]{1,0:T(8,128)S(1)} %bitcast.61), channel_id=1, source_target_pairs={{0,4},{4,8},{8,12},{12,0},{1,5},{5,9},{9,13},{13,1},{2,6},{6,10},{... | collective-permute-start | bytes 393224 | tf_op jit(solution)/shard_map/ppermute | solution.py:312
  55.8 2.0 %collective-permute-start.4 = (f32[512,256]{1,0:T(8,128)S(1)}, f32[512,256]{1,0:T(8,128)S(1)}, u32[]{:S(2)}, u32[]{:S(2)}) collective-permute-start(f32[512,256]{1,0:T(8,128)S(1)} %bitcast.57), channel_id=1, source_target_pairs={{0,1},{1,0},{2,3},{3,2},{4,5},{5,4},{6,7},{7,6},{8,9},{9,8},{10,11... | collective-permute-start | bytes 1572872 | tf_op jit(solution)/shard_map/ppermute | solution.py:312
  55.9 37.0 %copy-start = (bf16[288,256]{1,0:T(8,128)(2,1)S(1)}, bf16[288,256]{1,0:T(8,128)(2,1)}, u32[]{:S(2)}) copy-start(bf16[288,256]{1,0:T(8,128)(2,1)} %plane_ref.1) | copy-start | bytes 442372
  129.2 2.3 %collective-permute-start.9 = (bf16[1024,256]{1,0:T(8,128)(2,1)S(1)}, bf16[1024,256]{1,0:T(8,128)(2,1)S(1)}, u32[]{:S(2)}, u32[]{:S(2)}) collective-permute-start(bf16[1024,256]{1,0:T(8,128)(2,1)S(1)} %slice.4), channel_id=1, source_target_pairs={{0,1},{1,0},{2,3},{3,2},{4,5},{5,4},{6,7},{7,6},{8,9},{9,8},{10,11... | collective-permute-start | bytes 1572872 | tf_op jit(solution)/shard_map/ppermute | solution.py:312
